TPU v7x, 256 devices: a whole 4x4x8 slice. The times are simulated.
256 devices in a mesh: gx: 64 (over z_lo, x, y, core), gy: 4 (over z_hi).
Axes of the slice: x: 4, y: 4, z: 8 (z_hi: 4, z_lo: 2; z = z_hi * 2 + z_lo), core: 2. Of those that a mesh axis runs over, the one named last changes fastest.
Arguments:
- flow_state: float32 [5, 512, 64, 128], P(None, 'gx', 'gy'), may hold values from -3 to 13
- cotangent: float32 [5, 512, 64, 128], P(None, 'gx', 'gy'), may hold values from -6 to 6
- clip_flags: int32 [64, 8, 16], P('gx', 'gy'), may hold values from 0 to 2
- successor_ids: int32 [16], replicated, may hold values from 0 to 15, as said below
Outputs:
- residual: float32 [5, 512, 64, 128], P(None, 'gx', 'gy')
- grad_state: float32 [5, 512, 64, 128], P(None, 'gx', 'gy')
Inputs may be any that keep to these rules, and one draw needn't show every extreme that they name: Following successor_ids from any slot visits all 16 slots once before it returns.
All inputs are finite; a program needn't handle non-finite values.
Results may differ from a plain program's by a relative error of at most 0.0003.
Values sent between devices are 32-bit elements; how exact they have to be, the bound alone decides.
No kernel may reach another device: no remote copies, remote signals or barrier semaphores. Data moves between devices by JAX's collectives and lax.ppermute only.
A program may use at most 128 MiB of HBM per device.

v0:
```python
import functools

import jax
import jax.numpy as jnp
import numpy as np
from jax import lax
from jax.experimental import pallas as pl
from jax.experimental.pallas import tpu as pltpu
from jax.sharding import PartitionSpec as P
from numpy.polynomial import chebyshev, polynomial

F32 = jnp.float32
HIGHEST = lax.Precision.HIGHEST
EPS = 1e-05
PERMS = ((0, 1, 2), (1, 0, 2), (2, 0, 1))
NQ = 13
ROWS = 128


def legendre_values(points, node_count):
    values_table = np.zeros((points.shape[0], node_count))
    values_table[:, 0] = 1.0
    values_table[:, 1] = points
    for degree_index in range(2, node_count):
        values_table[:, degree_index] = (
            (2 * degree_index - 1) * points * values_table[:, degree_index - 1]
            - (degree_index - 1) * values_table[:, degree_index - 2]
        ) / degree_index
    return values_table


def node_tables():
    degree = 7
    node_count = degree + 1
    points = -np.cos(np.pi * np.arange(node_count) / degree)
    for newton_step in range(60):
        legend = legendre_values(points, node_count)
        points = points - (points * legend[:, degree] - legend[:, degree - 1]) / (
            node_count * legend[:, degree]
        )
    legend = legendre_values(points, node_count)
    weights = 2.0 / (degree * node_count * legend[:, degree] * legend[:, degree])
    differ = np.zeros((node_count, node_count))
    for row_index in range(node_count):
        for col_index in range(node_count):
            if row_index != col_index:
                differ[row_index, col_index] = legend[row_index, degree] / (
                    legend[col_index, degree] * (points[row_index] - points[col_index])
                )
    norm_table = 2.0 / (2.0 * np.arange(node_count) + 1.0)
    norm_table[degree] = 2.0 / degree
    to_modal = legend.T * weights[None, :] / norm_table[:, None]
    return (weights, differ, to_modal)


WEIGHTS, DIFFER, TO_MODAL = node_tables()
INV_W = [float(1.0 / w) for w in WEIGHTS]
SKEW = 2.0 * DIFFER * WEIGHTS[:, None]


def fitted(function, top, degree):
    series = chebyshev.Chebyshev.interpolate(function, degree, domain=[0.0, top])
    return [float(np.float32(c)) for c in series.convert(kind=polynomial.Polynomial).coef]


def sinhc(square):
    root = np.sqrt(np.maximum(square, 1e-12))
    return np.sinh(root) / root


def sinhc_slope(square):
    root = np.sqrt(np.maximum(square, 1e-12))
    exact = (np.cosh(root) - np.sinh(root) / root) / (root * root)
    series = 1.0 / 3.0 + square / 30.0 + square**2 / 840.0 + square**3 / 45360.0
    return np.where(square < 1e-2, series, exact)


MEAN_R = fitted(sinhc, 3.0, 4)
SLOPE_R = fitted(sinhc_slope, 3.0, 3)
MEAN_B = fitted(sinhc, 12.0, 5)
SLOPE_B = fitted(sinhc_slope, 12.0, 5)


def horner(coeffs, value):
    total = coeffs[-1] * value + coeffs[-2]
    for c in coeffs[-3::-1]:
        total = total * value + c
    return total


def rcp(value):
    return 1.0 / value


def log_parts(density, pressure):
    inv = rcp(density)
    ratio = pressure * inv
    half_log = 0.5 * jnp.log(density)
    return (
        jnp.sqrt(density),
        half_log,
        jnp.sqrt(5.0 * ratio),
        half_log - 0.5 * jnp.log(pressure),
    )


class Node:
    def __init__(self, vel, pres, root, theta, cot):
        self.vel, self.pres, self.cot = vel, pres, cot
        density = root * root
        vn, v1, v2 = vel
        mom = [density * v for v in vel]
        self.square = vn * vn + v1 * v1 + v2 * v2
        energy = 2.5 * pres + (0.5 * density) * self.square
        self.state = [density] + mom + [energy]
        mn = mom[0]
        self.flux = [mn, mn * vn + pres, mn * v1, mn * v2, (energy + pres) * vn]
        self.sound = theta * float(np.sqrt(1.4 / 5.0))
        self.speed = jnp.abs(vn) + self.sound

    def pull(self, half, direct, speed_cot):
        density = self.state[0]
        vn, v1, v2 = self.vel
        grad = [direct[i] + half[i] * vn for i in range(5)]
        sign = jnp.where(vn >= 0.0, 1.0, -1.0)
        dvn = half[0] * self.state[0]
        for i in range(1, 5):
            dvn = dvn + half[i] * self.state[i]
        dvn = dvn + half[4] * self.pres + speed_cot * sign
        inv = rcp(density)
        part = (0.5 * speed_cot) * self.sound
        dpres = half[1] + half[4] * vn + part * rcp(self.pres)
        over = dvn * inv
        pull_e = 0.4 * dpres
        grad[0] = grad[0] - part * inv - over * vn + (0.5 * pull_e) * self.square
        grad[1] = grad[1] + over - pull_e * vn
        grad[2] = grad[2] - pull_e * v1
        grad[3] = grad[3] - pull_e * v2
        grad[4] = grad[4] + pull_e
        return grad


def face(low, up):
    jump = [b - a for a, b in zip(low.state, up.state)]
    weight = [b - a for a, b in zip(low.cot, up.cot)]
    half_speed = 0.25 * (low.speed + up.speed)
    flux = [0.5 * (a + b) - half_speed * j for a, b, j in zip(low.flux, up.flux, jump)]
    dot = weight[0] * jump[0]
    for i in range(1, 5):
        dot = dot + weight[i] * jump[i]
    direct = [half_speed * w for w in weight]
    return flux, weight, direct, -0.25 * dot


def kernel_volume(
    flow, cot, flags, kxy, kzt, group, spread, out, zends, modes, msg, nat, turned, lines, prod, gsum
):
    for x in range(8):
        for h in range(2):
            src = pl.ds(x * 16 + h * 8, 8)
            dst = pl.ds(h * 64 + x * 8, 8)
            density = flow[0, src, :]
            inv = rcp(density)
            mom = [flow[1 + i, src, :] for i in range(3)]
            vel = [m * inv for m in mom]
            kinetic = mom[0] * vel[0] + mom[1] * vel[1] + mom[2] * vel[2]
            pres = 0.4 * (flow[4, src, :] - 0.5 * kinetic)
            prod[dst, :] = density * pres
            parts = vel + [pres] + list(log_parts(density, pres))
            for q in range(8):
                nat[q, dst, :] = parts[q]
            for q in range(5):
                value = cot[q, src, :]
                nat[8 + q, dst, :] = 2.0 * value if q == 0 else value
    for q in range(NQ):
        turned[q] = jnp.transpose(nat[q])
    for d in range(3):
        perm = PERMS[d]
        order = [perm[0], perm[1], perm[2], 3, 4, 5, 6, 7, 8] + [9 + i for i in perm] + [12]
        source = nat if d < 2 else turned
        for q in range(NQ):
            for h in range(2):
                for k in range(8):
                    rows = pl.ds(h * 64 + 8 * k, 8) if d == 0 else pl.ds(h * 64 + k, 8, stride=8)
                    value = source[order[q], rows, :]
                    lines[d, q, pl.ds(h * 64 + 8 * k, 8), :] = value * INV_W[k] if q >= 8 else value
    for q in range(NQ):
        for end in range(2):
            for h in range(2):
                zends[q, pl.ds(end * 16 + h * 8, 8), :] = lines[2, q, pl.ds(h * 64 + 56 * end, 8), :]

    def one(step, carry):
        d = step // 2
        base = (step % 2) * 64

        def rows(k):
            return pl.ds(pl.multiple_of(base + 8 * k, 8), 8)

        for k in range(7):
            a = [lines[d, q, rows(k), :] for q in range(NQ)]
            acc = [None] * 11 if k == 0 else [out[d, q, rows(k), :] for q in range(11)]
            for j in range(k + 1, 8):
                skew = float(SKEW[k, j])
                b = [lines[d, q, rows(j), :] for q in range(NQ)]
                vn, v1, v2 = (a[i] + b[i] for i in range(3))
                delta = [a[8 + i] - b[8 + i] for i in range(5)]
                y = a[5] - b[5]
                square = y * y
                scale = (0.25 * skew) * (a[4] * b[4])
                mean = scale * horner(MEAN_R, square)
                slope = (scale * y) * horner(SLOPE_R, square)
                yb = a[7] - b[7]
                square_b = yb * yb
                quot = rcp(horner(MEAN_B, square_b))
                inv5 = (a[6] * b[6]) * quot
                tilt = yb * (horner(SLOPE_B, square_b) * quot)
                dot = a[0] * b[0] + a[1] * b[1] + a[2] * b[2] + inv5
                mass = mean * vn
                half = 0.5 * skew
                flux = [
                    mass,
                    mass * vn + half * (a[3] + b[3]),
                    mass * v1,
                    mass * v2,
                    mass * dot + half * (a[3] * b[0] + b[3] * a[0]),
                ]
                phi = delta[0] + delta[1] * vn + delta[2] * v1 + delta[3] * v2 + delta[4] * dot
                common = phi * mean + delta[1] * mass
                t = half * delta[4]
                u = half * delta[1]
                w = mass * delta[4]
                r1 = mass * delta[2]
                r2 = mass * delta[3]
                pp = phi * mass
                qq = (phi * vn) * slope
                xx = w * inv5
                zz = xx * tilt
                grad_a = [
                    pp + qq,
                    common + w * b[0] + t * b[3],
                    r1 + w * b[1],
                    r2 + w * b[2],
                    u + t * b[0],
                    xx + zz,
                ]
                grad_b = [
                    pp - qq,
                    common + w * a[0] + t * a[3],
                    r1 + w * a[1],
                    r2 + w * a[2],
                    u + t * a[0],
                    xx - zz,
                ]
                for q in range(5):
                    acc[q] = flux[q] if acc[q] is None else acc[q] + flux[q]
                    before = 0.0 if k == 0 else out[d, q, rows(j), :]
                    out[d, q, rows(j), :] = before - flux[q]
                for q in range(6):
                    acc[5 + q] = grad_a[q] if acc[5 + q] is None else acc[5 + q] + grad_a[q]
                    out[d, 5 + q, rows(j), :] = grad_b[q] if k == 0 else out[d, 5 + q, rows(j), :] + grad_b[q]
            for q in range(11):
                out[d, q, rows(k), :] = acc[q]

        low = None
        zero = jnp.zeros((8, 128), F32)
        low_flux, low_weight, low_direct, low_dot = [zero] * 5, [zero] * 5, [zero] * 5, zero
        gained = zero
        for k in range(9):
            if k < 8:
                a = [lines[d, q, rows(k), :] for q in range(NQ)]
                node = Node(a[0:3], a[3], a[4], a[6], [0.5 * a[8]] + a[9:13])
            if k == 0:
                low = node
                continue
            if k < 8:
                flux, weight, direct, dot = face(low, node)
            else:
                flux, weight, direct, dot = [zero] * 5, [zero] * 5, [zero] * 5, zero
            m = k - 1
            total = [out[d, q, rows(m), :] for q in range(11)]
            total[0] = 2.0 * total[0]
            for q in range(5):
                diff = total[q] - (flux[q] - low_flux[q])
                gained = gained + low.cot[q] * diff
                out[d, q, rows(m), :] = total[q] * (-INV_W[m])
                out[d, 5 + q, rows(m), :] = diff * INV_W[m]
            fv = low.pull(
                [0.5 * (x + z) for x, z in zip(low_weight, weight)],
                [x - z for x, z in zip(direct, low_direct)],
                low_dot + dot,
            )
            inv = rcp(low.state[0])
            beta = 0.5 * total[10]
            g_rho = (beta - 0.5 * total[5]) * inv
            g_e = -0.4 * (total[9] + beta * rcp(low.pres))
            g_m = [-(total[6 + i] * inv) - g_e * low.vel[i] for i in range(3)]
            inner = g_m[0] * low.vel[0] + g_m[1] * low.vel[1] + g_m[2] * low.vel[2]
            dg = [g_rho - inner - (0.5 * g_e) * low.square] + g_m + [g_e]
            for q in range(5):
                out[d, 10 + q, rows(m), :] = dg[q]
                out[d, 15 + q, rows(m), :] = fv[q] - dg[q]
            low, low_flux, low_weight, low_direct, low_dot = node, flux, weight, direct, dot
        gsum[step] = gained
        return carry

    lax.fori_loop(0, 6, one, 0)

    coeffs = jnp.dot(kxy[...], prod[...], precision=HIGHEST, preferred_element_type=F32)
    coeffs = jnp.dot(coeffs, kzt[...], precision=HIGHEST, preferred_element_type=F32)
    modes[...] = coeffs
    squares = coeffs * coeffs
    sub = lax.broadcasted_iota(jnp.int32, (8, 128), 0)
    lane = lax.broadcasted_iota(jnp.int32, (8, 128), 1)
    high = (sub >= 6) | ((lane & 7) >= 6)
    packed = jnp.zeros((8, 128), F32)
    tops, alls, gains = [], [], []
    for h in range(2):
        every = squares[h * 64 : h * 64 + 8]
        for x in range(1, 6):
            every = every + squares[h * 64 + 8 * x : h * 64 + 8 * x + 8]
        ends = squares[h * 64 + 48 : h * 64 + 56] + squares[h * 64 + 56 : h * 64 + 64]
        tops.append(jnp.sum(jnp.where(high, every, 0.0) + ends, axis=0, keepdims=True))
        alls.append(jnp.sum(every + ends, axis=0, keepdims=True))
        gains.append(jnp.sum(gsum[h] + gsum[2 + h], axis=0, keepdims=True))
    for i, row in enumerate(tops + alls + gains):
        packed = jnp.where(sub == i, row, packed)
    sums = jnp.dot(packed, group[...], precision=HIGHEST, preferred_element_type=F32)
    along = jnp.concatenate([gsum[4], gsum[5]], axis=0)
    left = jnp.where(((sub == 4) & (lane < 64)) | ((sub == 5) & (lane >= 64)), 1.0, 0.0)
    per_slot = lax.dot_general(
        left, along, (((1,), (1,)), ((), ())), precision=HIGHEST, preferred_element_type=F32
    )
    sums = sums + jnp.dot(per_slot, spread[...], precision=HIGHEST, preferred_element_type=F32)
    flag_rows = jnp.dot(
        flags[...].astype(F32), spread[...], precision=HIGHEST, preferred_element_type=F32
    )
    packed = jnp.zeros((16, 128), F32)
    sub16 = lax.broadcasted_iota(jnp.int32, (16, 128), 0)
    for h in range(2):
        top = sums[h : h + 1] + EPS
        every = 0.01 * (sums[2 + h : 3 + h] + EPS)
        gain = sums[4 + h : 5 + h]
        flag = flag_rows[h : h + 1]
        over = rcp(top + every)
        keep = flag < 0.5
        alpha = jnp.where(keep, 0.5 * top * over, jnp.where(flag > 1.5, 0.5, 0.0))
        d_top = jnp.where(keep, every * over * over, 0.0)
        d_all = jnp.where(keep, -0.01 * top * over * over, 0.0)
        for i, row in enumerate((alpha, gain * (1.0 - alpha), gain, d_top, d_all)):
            packed = jnp.where(sub16 == 2 * i + h, row, packed)
    msg[...] = packed


def conserved_node(state, cot, direction):
    perm = PERMS[direction]
    density = state[0]
    inv = rcp(density)
    vel = [state[1 + i] * inv for i in perm]
    square = vel[0] * vel[0] + vel[1] * vel[1] + vel[2] * vel[2]
    pres = 0.4 * (state[4] - 0.5 * density * square)
    scaled = [cot[0]] + [cot[1 + i] for i in perm] + [cot[4]]
    return Node(vel, pres, jnp.sqrt(density), jnp.sqrt(5.0 * pres * inv), [c * INV_W[0] for c in scaled])


def face_shares(low, up):
    flux, weight, direct, dot = face(low, up)
    half = [0.5 * w for w in weight]
    return (
        [-INV_W[7] * f for f in flux],
        low.pull(half, direct, dot),
        [INV_W[0] * f for f in flux],
        up.pull(half, [-x for x in direct], dot),
    )


def kernel_faces(
    ids, flow, cot, x_left, x_right, y_left, y_right, parts, zends, modes, msg, kxyt, kz, base, extra, slope, zacc, znext, zback
):
    for k in range(16):
        znext[:, pl.ds(k, 1), :] = zends[:, pl.ds(ids[k], 1), :]
    for h in range(2):
        def side(ref, start):
            v = [ref[q, pl.ds(start + h * 8, 8), :] for q in range(NQ)]
            return Node(v[0:3], v[3], v[4], v[6], [0.5 * v[8]] + v[9:13])

        low_r, low_g, up_r, up_g = face_shares(side(zends, 16), side(znext, 0))
        for q in range(5):
            zacc[q, pl.ds(h * 8, 8), :] = low_r[q]
            zacc[5 + q, pl.ds(h * 8, 8), :] = low_g[q]
            zback[q, pl.ds(h * 8, 8), :] = up_r[q]
            zback[5 + q, pl.ds(h * 8, 8), :] = up_g[q]
    for k in range(16):
        zacc[:, pl.ds(16 + ids[k], 1), :] = zback[:, pl.ds(k, 1), :]

    def place(d, q):
        return q if q in (0, 4) else 1 + PERMS[d][q - 1]

    back = [[place(d, q) for q in range(5)] for d in range(3)]
    for group_at, target, offset in ((0, base, 0), (1, extra, 0), (2, base, 5), (3, extra, 5)):
        for q in range(5):
            first = group_at * 5
            qx = first + back[0].index(q)
            qy = first + back[1].index(q)
            qz = back[2].index(q)
            pieces = []
            for slot in range(16):
                h, s = slot // 8, slot % 8
                pieces.append(parts[2, first + qz, pl.ds(h * 64 + s, 8, stride=8), :])
            if group_at in (0, 2):
                source = qz + (0 if group_at == 0 else 5)
                sub = lax.broadcasted_iota(jnp.int32, (8, 128), 0)
                for slot in range(16):
                    upper = zacc[source, pl.ds(slot, 1), :]
                    lower = zacc[source, pl.ds(16 + slot, 1), :]
                    add = jnp.where(sub == 7, upper, jnp.where(sub == 0, lower, 0.0))
                    pieces[slot] = pieces[slot] + add
            whole = jnp.transpose(jnp.concatenate(pieces, axis=0))
            for h in range(2):
                for x in range(8):
                    value = (
                        parts[0, qx, pl.ds(h * 64 + 8 * x, 8), :]
                        + parts[1, qy, pl.ds(h * 64 + x, 8, stride=8), :]
                        + whole[h * 64 + 8 * x : h * 64 + 8 * x + 8]
                    )
                    target[offset + q, pl.ds(x * 16 + h * 8, 8), :] = value

    def own(direction, rows):
        return conserved_node([flow[q, rows, :] for q in range(5)], [cot[q, rows, :] for q in range(5)], direction)

    def add(direction, rows, res, grad):
        for q in range(5):
            p = place(direction, q)
            base[p, rows, :] += res[q]
            base[5 + p, rows, :] += grad[q]

    def near(ref, rows, direction):
        return conserved_node([ref[q, rows, :] for q in range(5)], [ref[5 + q, rows, :] for q in range(5)], direction)

    for h in range(2):
        here = pl.ds(h * 8, 8)
        top = pl.ds(112 + h * 8, 8)
        low_r, low_g, up_r, up_g = face_shares(near(x_left, here, 0), own(0, here))
        add(0, here, up_r, up_g)
        low_r, low_g, up_r, up_g = face_shares(own(0, top), near(x_right, here, 0))
        add(0, top, low_r, low_g)
    whole = pl.ds(0, 8)
    rows = [pl.ds(k, 8, stride=16) for k in (0, 7, 8, 15)]
    low_r, low_g, up_r, up_g = face_shares(near(y_left, whole, 1), own(1, rows[0]))
    add(1, rows[0], up_r, up_g)
    low_r, low_g, up_r, up_g = face_shares(own(1, rows[1]), own(1, rows[2]))
    add(1, rows[1], low_r, low_g)
    add(1, rows[2], up_r, up_g)
    low_r, low_g, up_r, up_g = face_shares(own(1, rows[3]), near(y_right, whole, 1))
    add(1, rows[3], low_r, low_g)

    sub = lax.broadcasted_iota(jnp.int32, (8, 128), 0)
    lane = lax.broadcasted_iota(jnp.int32, (8, 128), 1)
    high = (sub >= 6) | ((lane & 7) >= 6)
    tiles = []
    for h in range(2):
        d_top = msg[pl.ds(6 + h, 1), :]
        d_all = msg[pl.ds(8 + h, 1), :]
        both = d_top + d_all
        mixed = jnp.where(high, both, d_all)
        for x in range(8):
            tiles.append(modes[pl.ds(h * 64 + 8 * x, 8), :] * (both if x >= 6 else mixed))
    weighed = jnp.concatenate(tiles, axis=0)
    weighed = jnp.dot(kxyt[...], weighed, precision=HIGHEST, preferred_element_type=F32)
    weighed = jnp.dot(weighed, kz[...], precision=HIGHEST, preferred_element_type=F32)
    for h in range(2):
        for x in range(8):
            rows = pl.ds(x * 16 + h * 8, 8)
            density = flow[0, rows, :]
            inv = rcp(density)
            vel = [flow[1 + i, rows, :] * inv for i in range(3)]
            square = vel[0] * vel[0] + vel[1] * vel[1] + vel[2] * vel[2]
            pres = 0.4 * (flow[4, rows, :] - 0.5 * density * square)
            value = weighed[h * 64 + 8 * x : h * 64 + 8 * x + 8]
            pull_e = 0.4 * (value * density)
            slope[0, rows, :] = value * pres + (0.5 * pull_e) * square
            for i in range(3):
                slope[1 + i, rows, :] = -(pull_e * vel[i])
            slope[4, rows, :] = pull_e


def kernel_blend(ids, msg, from_left, from_right, from_low, from_up, base, extra, slope, residual, grad):
    row = lax.broadcasted_iota(jnp.int32, (128, 128), 0)
    lane = lax.broadcasted_iota(jnp.int32, (128, 128), 1)
    slot = lane >> 3
    above = jnp.zeros((128, 128), jnp.int32)
    for k in range(16):
        above = jnp.where(slot == k, ids[k], above)
    up = jnp.where((above * 8 + (lane & 7)) == row, 1.0, 0.0)
    own = msg[0:8, :]
    beside = jnp.dot(own, up, precision=HIGHEST, preferred_element_type=F32) + lax.dot_general(
        own, up, (((1,), (1,)), ((), ())), precision=HIGHEST, preferred_element_type=F32
    )
    beside = beside + from_left[0:8, :] + from_right[0:8, :]
    for h in range(2):
        def beside_of(i):
            low = from_low[2 * i + 1 : 2 * i + 2, :] if h == 0 else msg[2 * i : 2 * i + 1, :]
            high = msg[2 * i + 1 : 2 * i + 2, :] if h == 0 else from_up[2 * i : 2 * i + 1, :]
            return beside[2 * i + h : 2 * i + h + 1, :] + low + high

        alpha = msg[h : h + 1, :]
        gain = msg[4 + h : 5 + h, :]
        around = beside_of(0)
        smooth = alpha + (1.0 - alpha) * around * (0.5 / 6.0)
        pull = gain * (1.0 - around * (0.5 / 6.0)) + beside_of(1) * (0.5 / 6.0)
        smooth = jnp.broadcast_to(smooth, (8, 128))
        pull = jnp.broadcast_to(pull, (8, 128))
        for x in range(8):
            rows = pl.ds(x * 16 + h * 8, 8)
            for q in range(5):
                residual[q, rows, :] = base[q, rows, :] + smooth * extra[q, rows, :]
                grad[q, rows, :] = (
                    base[5 + q, rows, :] + smooth * extra[5 + q, rows, :] + pull * slope[q, rows, :]
                )


def shifted(value, axis, steps):
    count = lax.axis_size(axis)
    return lax.ppermute(value, axis, [(i, (i + steps) % count) for i in range(count)])


def shape(*dims):
    return jax.ShapeDtypeStruct(dims, F32)


def shards(flow_state, cotangent, clip_flags, successor_ids):
    flow = flow_state.reshape(5, ROWS, 128)
    cot = cotangent.reshape(5, ROWS, 128)
    vmem = pl.BlockSpec(memory_space=pltpu.VMEM)
    smem = pl.BlockSpec(memory_space=pltpu.SMEM)
    params = pltpu.CompilerParams(vmem_limit_bytes=48 * 1024 * 1024)

    both = jnp.concatenate([flow_state, cotangent], axis=0)
    x_left = shifted(both[:, 7], "gx", 1)
    x_right = shifted(both[:, 0], "gx", -1)
    y_left = shifted(both[:, :, 15], "gy", 1)
    y_right = shifted(both[:, :, 0], "gy", -1)

    modal = np.asarray(TO_MODAL, np.float32)
    kxy = np.kron(np.eye(2), np.kron(modal, modal)).astype(np.float32)
    kz = np.kron(np.eye(16), modal).astype(np.float32)
    group = np.kron(np.eye(16), np.ones((8, 8))).astype(np.float32)
    spread = np.kron(np.eye(16), np.ones((1, 8))).astype(np.float32)

    parts, zends, modes, msg = pl.pallas_call(
        kernel_volume,
        out_shape=(shape(3, 20, ROWS, 128), shape(NQ, 32, 128), shape(ROWS, 128), shape(16, 128)),
        in_specs=[vmem] * 7,
        out_specs=[vmem] * 4,
        scratch_shapes=[
            pltpu.VMEM((NQ, ROWS, 128), F32),
            pltpu.VMEM((NQ, ROWS, 128), F32),
            pltpu.VMEM((3, NQ, ROWS, 128), F32),
            pltpu.VMEM((ROWS, 128), F32),
            pltpu.VMEM((6, 8, 128), F32),
        ],
        compiler_params=params,
        name="volume",
    )(flow, cot, clip_flags.reshape(2, 16), kxy, np.ascontiguousarray(kz.T), group, spread)

    sent = msg[0:8]
    from_left = shifted(sent, "gx", 1)
    from_right = shifted(sent, "gx", -1)
    from_low = shifted(sent, "gy", 1)
    from_up = shifted(sent, "gy", -1)

    base, extra, slope = pl.pallas_call(
        kernel_faces,
        out_shape=(shape(10, ROWS, 128), shape(10, ROWS, 128), shape(5, ROWS, 128)),
        in_specs=[smem] + [vmem] * 12,
        out_specs=[vmem] * 3,
        scratch_shapes=[
            pltpu.VMEM((10, 32, 128), F32),
            pltpu.VMEM((NQ, 16, 128), F32),
            pltpu.VMEM((10, 16, 128), F32),
        ],
        compiler_params=params,
        name="faces",
    )(
        successor_ids, flow, cot, x_left, x_right, y_left, y_right, parts, zends, modes, msg,
        np.ascontiguousarray(kxy.T), kz,
    )

    residual, grad = pl.pallas_call(
        kernel_blend,
        out_shape=(shape(5, ROWS, 128), shape(5, ROWS, 128)),
        in_specs=[smem] + [vmem] * 8,
        out_specs=[vmem] * 2,
        compiler_params=params,
        name="blend",
    )(successor_ids, msg, from_left, from_right, from_low, from_up, base, extra, slope)
    return residual.reshape(flow_state.shape), grad.reshape(flow_state.shape)


def solution(mesh):
    placed = P(None, "gx", "gy", None)
    return jax.shard_map(
        shards,
        mesh=mesh,
        in_specs=(placed, placed, P("gx", "gy", None), P()),
        out_specs=(placed, placed),
        check_vma=False,
    )
```

profile of v0, /device:TPU:1, one launch (start us, length us, event | category | flops | bytes accessed | tf_op | source)
XLA Modules:
  0.0 42.2 jit_solution(4514820757355948401)
XLA Ops:
  0.6 1.1 %copy_dynamic-update-slice_fusion.1 = f32[10,8,16,128]{3,1,0,2:T(8,128)S(1)} fusion(f32[5,8,16,128]{3,2,1,0:T(8,128)} %param.10), kind=kLoop, calls=%fused_computation.1 | loop fusion | bytes 655360
  1.7 1.1 %copy_dynamic-update-slice_fusion = f32[10,8,16,128]{3,1,0,2:T(8,128)S(1)} fusion(f32[10,8,16,128]{3,1,0,2:T(8,128)S(1)} %copy_dynamic-update-slice_fusion.1, f32[5,8,16,128]{3,2,1,0:T(8,128)} %param.11), kind=kLoop, calls=%fused_computation | loop fusion | bytes 655360 | tf_op jit(solution)/shard_map/concatenate | solution.py:537
  2.8 0.1 fusion
  2.9 2.8 %collective-permute-start.4 = (f32[10,16,128]{2,1,0:T(8,128)S(1)}, f32[10,16,128]{2,1,0:T(8,128)S(1)}, u32[]{:S(2)}, u32[]{:S(2)}) collective-permute-start(f32[10,16,128]{2,1,0:T(8,128)S(1)} %bitcast.21), channel_id=1, source_target_pairs={{0,4},{4,8},{8,12},{12,16},{16,20},{20,24},{24,28},{28,32},{32,36}... | collective-permute-start | bytes 245768 | tf_op jit(solution)/shard_map/ppermute | solution.py:523
  5.7 0.7 %collective-permute-start.5 = (f32[10,16,128]{2,1,0:T(8,128)S(1)}, f32[10,16,128]{2,1,0:T(8,128)S(1)}, u32[]{:S(2)}, u32[]{:S(2)}) collective-permute-start(f32[10,16,128]{2,1,0:T(8,128)S(1)} %bitcast.20), channel_id=1, source_target_pairs={{0,252},{4,0},{8,4},{12,8},{16,12},{20,16},{24,20},{28,24},{32,28}... | collective-permute-start | bytes 245768 | tf_op jit(solution)/shard_map/ppermute | solution.py:523
  6.3 5.5 %collective-permute-start.7 = (f32[10,8,128]{2,1,0:T(8,128)S(1)}, f32[10,8,128]{2,1,0:T(8,128)S(1)}, u32[]{:S(2)}, u32[]{:S(2)}) collective-permute-start(f32[10,8,128]{2,1,0:T(8,128)S(1)} %get-tuple-element.20), channel_id=1, source_target_pairs={{0,3},{1,0},{2,1},{3,2},{4,7},{5,4},{6,5},{7,6},{8,11},{9,8},{10,9... | collective-permute-start | bytes 122888 | tf_op jit(solution)/shard_map/ppermute | solution.py:523
  11.8 0.0 collective-permute-start.6
  11.8 1.0 %copy-done.1 = f32[5,8,16,128]{3,2,1,0:T(8,128)S(1)} copy-done((f32[5,8,16,128]{3,2,1,0:T(8,128)S(1)}, f32[5,8,16,128]{3,2,1,0:T(8,128)}, u32[]{:S(2)}) %copy-start.1) | copy-done | bytes 327704
  12.8 1.0 %copy-done.2 = f32[5,8,16,128]{3,2,1,0:T(8,128)S(1)} copy-done((f32[5,8,16,128]{3,2,1,0:T(8,128)S(1)}, f32[5,8,16,128]{3,2,1,0:T(8,128)}, u32[]{:S(2)}) %copy-start.2) | copy-done | bytes 327704
  13.8 0.8 %copy-done.5 = f32[128,128]{1,0:T(8,128)S(1)} copy-done((f32[128,128]{1,0:T(8,128)S(1)}, f32[128,128]{1,0:T(8,128)}, u32[]{:S(2)}) %copy-start.5) | copy-done | bytes 65560
  14.6 0.8 %copy-done.6 = f32[128,128]{1,0:T(8,128)S(1)} copy-done((f32[128,128]{1,0:T(8,128)S(1)}, f32[128,128]{1,0:T(8,128)}, u32[]{:S(2)}) %copy-start.6) | copy-done | bytes 65560
  15.4 0.8 %copy-done.7 = f32[128,128]{1,0:T(8,128)S(1)} copy-done((f32[128,128]{1,0:T(8,128)S(1)}, f32[128,128]{1,0:T(8,128)}, u32[]{:S(2)}) %copy-start.7) | copy-done | bytes 65560
  16.3 0.7 %copy-done.8 = f32[16,128]{1,0:T(8,128)S(1)} copy-done((f32[16,128]{1,0:T(8,128)S(1)}, f32[16,128]{1,0:T(8,128)}, u32[]{:S(2)}) %copy-start.8) | copy-done | bytes 8216
  17.0 0.7 %copy-done.10 = s32[1,2,16]{2,1,0:T(2,128)S(1)} copy-done((s32[1,2,16]{2,1,0:T(2,128)S(1)}, s32[1,2,16]{2,1,0:T(2,128)}, u32[]{:S(2)}) %copy-start.10) | copy-done | bytes 152
  17.7 6.1 %volume.1 = (f32[3,20,128,128]{3,2,1,0:T(8,128)S(1)}, f32[13,32,128]{2,1,0:T(8,128)S(1)}, f32[128,128]{1,0:T(8,128)S(1)}, f32[16,128]{1,0:T(8,128)S(1)}) custom-call(f32[5,128,128]{2,1,0:T(8,128)S(1)} %bitcast.15, f32[5,128,128]{2,1,0:T(8,128)S(1)} %bitcast.17, s32[2,16]{1,0:T(2,128)S(1)} %bitcast.19, f32[128,128]{1,0:T(8,128)S(1)} %copy-done.7, ...), custom_call_target="tpu_custom_call" | custom-call | tf_op jit(solution)/shard_map/volume/pallas_call | solution.py:549
  23.8 1.9 %copy-done = f32[3,20,128,128]{3,2,1,0:T(8,128)} copy-done((f32[3,20,128,128]{3,2,1,0:T(8,128)}, f32[3,20,128,128]{3,2,1,0:T(8,128)S(1)}, u32[]{:S(2)}) %copy-start) | copy-done | bytes 3932184
  25.6 3.6 %collective-permute-start.3 = (f32[8,128]{1,0:T(8,128)S(1)}, f32[8,128]{1,0:T(8,128)S(1)}, u32[]{:S(2)}, u32[]{:S(2)}) collective-permute-start(f32[8,128]{1,0:T(8,128)S(1)} %slice.15), channel_id=1, source_target_pairs={{0,3},{1,0},{2,1},{3,2},{4,7},{5,4},{6,5},{7,6},{8,11},{9,8},{10,9... | collective-permute-start | bytes 12296 | tf_op jit(solution)/shard_map/ppermute | solution.py:523
  29.2 0.0 collective-permute-done.7.y_right
  29.2 0.0 collective-permute-start.2
  29.2 0.0 collective-permute-done.6.y_left
  29.2 5.6 %collective-permute-start.1 = (f32[8,128]{1,0:T(8,128)S(1)}, f32[8,128]{1,0:T(8,128)S(1)}, u32[]{:S(2)}, u32[]{:S(2)}) collective-permute-start(f32[8,128]{1,0:T(8,128)S(1)} %slice.15), channel_id=1, source_target_pairs={{0,252},{4,0},{8,4},{12,8},{16,12},{20,16},{24,20},{28,24},{32,28}... | collective-permute-start | bytes 12296 | tf_op jit(solution)/shard_map/ppermute | solution.py:523
  34.8 0.0 collective-permute-done.4.x_left
  34.8 0.0 collective-permute-start
  34.8 0.0 collective-permute-done.5.x_right
  34.8 0.0 copy-start.3
  34.8 0.8 %copy-done.3 = f32[128,128]{1,0:T(8,128)S(1)} copy-done((f32[128,128]{1,0:T(8,128)S(1)}, f32[128,128]{1,0:T(8,128)}, u32[]{:S(2)}) %copy-start.3) | copy-done | bytes 65560
  35.7 0.8 %copy-done.4 = f32[128,128]{1,0:T(8,128)S(1)} copy-done((f32[128,128]{1,0:T(8,128)S(1)}, f32[128,128]{1,0:T(8,128)}, u32[]{:S(2)}) %copy-start.4) | copy-done | bytes 65560
  36.5 0.7 %copy-done.9 = s32[16]{0:T(128)S(1)} copy-done((s32[16]{0:T(128)S(1)}, s32[16]{0:T(128)}, u32[]{:S(2)}) %copy-start.9) | copy-done | bytes 88
  37.2 3.3 %faces.1 = (f32[10,128,128]{2,1,0:T(8,128)S(1)}, f32[10,128,128]{2,1,0:T(8,128)S(1)}, f32[5,128,128]{2,1,0:T(8,128)S(1)}) custom-call(s32[16]{0:T(128)S(1)} %copy-done.9, f32[5,128,128]{2,1,0:T(8,128)S(1)} %bitcast.16, f32[5,128,128]{2,1,0:T(8,128)S(1)} %bitcast.18, f32[10,16,128]{2,1,0:T(8,128)S(1)} %collective-permute-done.4.x_left, ...), custom_call_target="tpu_custom_call" | custom-call | tf_op jit(solution)/shard_map/faces/pallas_call | solution.py:571
  40.5 0.0 collective-permute-done.3.from_up
  40.5 0.0 collective-permute-done.from_left
  40.5 1.7 %blend.1 = (f32[5,128,128]{2,1,0:T(8,128)}, f32[5,128,128]{2,1,0:T(8,128)}) custom-call(s32[16]{0:T(128)S(1)} %copy-done.9, f32[16,128]{1,0:T(8,128)S(1)} %get-tuple-element.11.msg, f32[8,128]{1,0:T(8,128)S(1)} %collective-permute-done.from_left, f32[8,128]{1,0:T(8,128)S(1)} %collective-permute-done.1.from_right, ...), custom_call_target="tpu_custom_call" | custom-call | tf_op jit(solution)/shard_map/blend/pallas_call | solution.py:588
  (16 shorter events, 0.0 us)
Async XLA Ops:
  2.9 31.9 %collective-permute-start.4 = (f32[10,16,128]{2,1,0:T(8,128)S(1)}, f32[10,16,128]{2,1,0:T(8,128)S(1)}, u32[]{:S(2)}, u32[]{:S(2)}) collective-permute-start(f32[10,16,128]{2,1,0:T(8,128)S(1)} %bitcast.21), channel_id=1, source_target_pairs={{0,4},{4,8},{8,12},{12,16},{16,20},{20,24},{24,28},{28,32},{32,36}... | collective-permute-start | bytes 245768 | tf_op jit(solution)/shard_map/ppermute | solution.py:523
  5.7 29.1 %collective-permute-start.5 = (f32[10,16,128]{2,1,0:T(8,128)S(1)}, f32[10,16,128]{2,1,0:T(8,128)S(1)}, u32[]{:S(2)}, u32[]{:S(2)}) collective-permute-start(f32[10,16,128]{2,1,0:T(8,128)S(1)} %bitcast.20), channel_id=1, source_target_pairs={{0,252},{4,0},{8,4},{12,8},{16,12},{20,16},{24,20},{28,24},{32,28}... | collective-permute-start | bytes 245768 | tf_op jit(solution)/shard_map/ppermute | solution.py:523
  6.3 22.9 %collective-permute-start.7 = (f32[10,8,128]{2,1,0:T(8,128)S(1)}, f32[10,8,128]{2,1,0:T(8,128)S(1)}, u32[]{:S(2)}, u32[]{:S(2)}) collective-permute-start(f32[10,8,128]{2,1,0:T(8,128)S(1)} %get-tuple-element.20), channel_id=1, source_target_pairs={{0,3},{1,0},{2,1},{3,2},{4,7},{5,4},{6,5},{7,6},{8,11},{9,8},{10,9... | collective-permute-start | bytes 122888 | tf_op jit(solution)/shard_map/ppermute | solution.py:523
  11.8 17.4 %collective-permute-start.6 = (f32[10,8,128]{2,1,0:T(8,128)S(1)}, f32[10,8,128]{2,1,0:T(8,128)S(1)}, u32[]{:S(2)}, u32[]{:S(2)}) collective-permute-start(f32[10,8,128]{2,1,0:T(8,128)S(1)} %get-tuple-element.21), channel_id=1, source_target_pairs={{0,1},{1,2},{2,3},{3,0},{4,5},{5,6},{6,7},{7,4},{8,9},{9,10},{10,1... | collective-permute-start | bytes 122888 | tf_op jit(solution)/shard_map/ppermute | solution.py:523
  11.8 1.0 %copy-start.1 = (f32[5,8,16,128]{3,2,1,0:T(8,128)S(1)}, f32[5,8,16,128]{3,2,1,0:T(8,128)}, u32[]{:S(2)}) copy-start(f32[5,8,16,128]{3,2,1,0:T(8,128)} %param.10) | copy-start | bytes 983044
  12.8 1.0 %copy-start.2 = (f32[5,8,16,128]{3,2,1,0:T(8,128)S(1)}, f32[5,8,16,128]{3,2,1,0:T(8,128)}, u32[]{:S(2)}) copy-start(f32[5,8,16,128]{3,2,1,0:T(8,128)} %param.11) | copy-start | bytes 983044
  13.8 0.8 %copy-start.5 = (f32[128,128]{1,0:T(8,128)S(1)}, f32[128,128]{1,0:T(8,128)}, u32[]{:S(2)}) copy-start(f32[128,128]{1,0:T(8,128)} %constant.14.clone.group) | copy-start | bytes 196612
  14.6 0.8 %copy-start.6 = (f32[128,128]{1,0:T(8,128)S(1)}, f32[128,128]{1,0:T(8,128)}, u32[]{:S(2)}) copy-start(f32[128,128]{1,0:T(8,128)} %constant.13.clone.kzt) | copy-start | bytes 196612
  15.4 0.8 %copy-start.7 = (f32[128,128]{1,0:T(8,128)S(1)}, f32[128,128]{1,0:T(8,128)}, u32[]{:S(2)}) copy-start(f32[128,128]{1,0:T(8,128)} %constant.12.clone.kxy) | copy-start | bytes 196612
  16.3 0.7 %copy-start.8 = (f32[16,128]{1,0:T(8,128)S(1)}, f32[16,128]{1,0:T(8,128)}, u32[]{:S(2)}) copy-start(f32[16,128]{1,0:T(8,128)} %constant.15.clone.spread) | copy-start | bytes 24580
  17.0 0.7 %copy-start.10 = (s32[1,2,16]{2,1,0:T(2,128)S(1)}, s32[1,2,16]{2,1,0:T(2,128)}, u32[]{:S(2)}) copy-start(s32[1,2,16]{2,1,0:T(2,128)} %param.12) | copy-start | bytes 388
  23.8 1.9 %copy-start = (f32[3,20,128,128]{3,2,1,0:T(8,128)}, f32[3,20,128,128]{3,2,1,0:T(8,128)S(1)}, u32[]{:S(2)}) copy-start(f32[3,20,128,128]{3,2,1,0:T(8,128)S(1)} %get-tuple-element.12.parts) | copy-start | bytes 11796484
  25.6 14.8 %collective-permute-start.3 = (f32[8,128]{1,0:T(8,128)S(1)}, f32[8,128]{1,0:T(8,128)S(1)}, u32[]{:S(2)}, u32[]{:S(2)}) collective-permute-start(f32[8,128]{1,0:T(8,128)S(1)} %slice.15), channel_id=1, source_target_pairs={{0,3},{1,0},{2,1},{3,2},{4,7},{5,4},{6,5},{7,6},{8,11},{9,8},{10,9... | collective-permute-start | bytes 12296 | tf_op jit(solution)/shard_map/ppermute | solution.py:523
  29.2 11.3 %collective-permute-start.2 = (f32[8,128]{1,0:T(8,128)S(1)}, f32[8,128]{1,0:T(8,128)S(1)}, u32[]{:S(2)}, u32[]{:S(2)}) collective-permute-start(f32[8,128]{1,0:T(8,128)S(1)} %slice.15), channel_id=1, source_target_pairs={{0,1},{1,2},{2,3},{3,0},{4,5},{5,6},{6,7},{7,4},{8,9},{9,10},{10,1... | collective-permute-start | bytes 12296 | tf_op jit(solution)/shard_map/ppermute | solution.py:523
  29.2 11.3 %collective-permute-start.1 = (f32[8,128]{1,0:T(8,128)S(1)}, f32[8,128]{1,0:T(8,128)S(1)}, u32[]{:S(2)}, u32[]{:S(2)}) collective-permute-start(f32[8,128]{1,0:T(8,128)S(1)} %slice.15), channel_id=1, source_target_pairs={{0,252},{4,0},{8,4},{12,8},{16,12},{20,16},{24,20},{28,24},{32,28}... | collective-permute-start | bytes 12296 | tf_op jit(solution)/shard_map/ppermute | solution.py:523
  34.8 5.7 %collective-permute-start = (f32[8,128]{1,0:T(8,128)S(1)}, f32[8,128]{1,0:T(8,128)S(1)}, u32[]{:S(2)}, u32[]{:S(2)}) collective-permute-start(f32[8,128]{1,0:T(8,128)S(1)} %slice.15), channel_id=1, source_target_pairs={{0,4},{4,8},{8,12},{12,16},{16,20},{20,24},{24,28},{28,32},{32,36}... | collective-permute-start | bytes 12296 | tf_op jit(solution)/shard_map/ppermute | solution.py:523
  34.8 0.8 %copy-start.3 = (f32[128,128]{1,0:T(8,128)S(1)}, f32[128,128]{1,0:T(8,128)}, u32[]{:S(2)}) copy-start(f32[128,128]{1,0:T(8,128)} %constant.17.clone.kz) | copy-start | bytes 196612
  35.7 0.8 %copy-start.4 = (f32[128,128]{1,0:T(8,128)S(1)}, f32[128,128]{1,0:T(8,128)}, u32[]{:S(2)}) copy-start(f32[128,128]{1,0:T(8,128)} %constant.16.clone.kxyt) | copy-start | bytes 196612
  36.5 0.7 %copy-start.9 = (s32[16]{0:T(128)S(1)}, s32[16]{0:T(128)}, u32[]{:S(2)}) copy-start(s32[16]{0:T(128)} %ids.3) | copy-start | bytes 196
where the time goes:
time: 42.8 us; the launch traced here: 42.2 us
  starting transfers between devices  18.1 us (42%)
  local copies, waits for them, and re-layouts  12.3 us (29%)
  Pallas kernels  11.1 us (26%)
  between operations  0.74 us (2%)
    ppermute x8, starting transfers between devices, shifted(): lax.ppermute(value, axis, [(i, (i + steps) % count) for i in range(count)])  18.1 us
    unnamed x23, local copies, waits for them, and re-layouts  11.1 us
    pallas_call x1, Pallas kernels, shards(): pl.pallas_call(kernel_volume, out_shape=(shape(3, 20, ROWS, 128), shape(N...  6.1 us
    pallas_call x1, Pallas kernels, shards(): pl.pallas_call(kernel_faces, out_shape=(shape(10, ROWS, 128), shape(10, R...  3.29 us
    pallas_call x1, Pallas kernels, shards(): pl.pallas_call(kernel_blend, out_shape=(shape(5, ROWS, 128), shape(5, ROW...  1.71 us
    concatenate x1, local copies, waits for them, and re-layouts, shards(): both = jnp.concatenate([flow_state, cotangent], axis=0)  1.07 us
  transfers between devices with their start and end apart: 8, of which 0 were waited for; matrix products, arithmetic and copies ran while one was open for 0% of the time, Pallas kernels for 22%

commit v1 on v0

--- a/solution.py
+++ b/solution.py
@@ -1,5 +1,3 @@
-import functools
-
 import jax
 import jax.numpy as jnp
 import numpy as np
@@ -153,8 +151,46 @@
 
 
 def kernel_volume(
-    flow, cot, flags, kxy, kzt, group, spread, out, zends, modes, msg, nat, turned, lines, prod, gsum
+    flow_hbm,
+    cot_hbm,
+    flags_hbm,
+    tables_hbm,
+    out,
+    zends,
+    modes,
+    msg,
+    to_right,
+    to_left,
+    to_up,
+    to_low,
+    flow,
+    cot,
+    tables,
+    nat,
+    turned,
+    lines,
+    prod,
+    gsum,
+    flags,
+    sems,
 ):
+    copies = [
+        pltpu.make_async_copy(source, target, sems.at[i])
+        for i, (source, target) in enumerate(
+            ((flow_hbm, flow), (cot_hbm, cot), (tables_hbm, tables), (flags_hbm, flags))
+        )
+    ]
+    for copy in copies:
+        copy.start()
+    copies[0].wait()
+    copies[1].wait()
+    for c in range(10):
+        source, q = (flow, c) if c < 5 else (cot, c - 5)
+        to_right[pl.ds(16 * c, 16), :] = source[q, pl.ds(112, 16), :]
+        to_left[pl.ds(16 * c, 16), :] = source[q, pl.ds(0, 16), :]
+        to_up[pl.ds(8 * c, 8), :] = source[q, pl.ds(15, 8, stride=16), :]
+        to_low[pl.ds(8 * c, 8), :] = source[q, pl.ds(0, 8, stride=16), :]
+
     for x in range(8):
         for h in range(2):
             src = pl.ds(x * 16 + h * 8, 8)
@@ -305,8 +341,10 @@
 
     lax.fori_loop(0, 6, one, 0)
 
-    coeffs = jnp.dot(kxy[...], prod[...], precision=HIGHEST, preferred_element_type=F32)
-    coeffs = jnp.dot(coeffs, kzt[...], precision=HIGHEST, preferred_element_type=F32)
+    copies[2].wait()
+    copies[3].wait()
+    coeffs = jnp.dot(tables[0], prod[...], precision=HIGHEST, preferred_element_type=F32)
+    coeffs = jnp.dot(coeffs, tables[1], precision=HIGHEST, preferred_element_type=F32)
     modes[...] = coeffs
     squares = coeffs * coeffs
     sub = lax.broadcasted_iota(jnp.int32, (8, 128), 0)
@@ -324,15 +362,27 @@
         gains.append(jnp.sum(gsum[h] + gsum[2 + h], axis=0, keepdims=True))
     for i, row in enumerate(tops + alls + gains):
         packed = jnp.where(sub == i, row, packed)
-    sums = jnp.dot(packed, group[...], precision=HIGHEST, preferred_element_type=F32)
+    group = jnp.where(
+        lax.broadcasted_iota(jnp.int32, (128, 128), 0) >> 3
+        == lax.broadcasted_iota(jnp.int32, (128, 128), 1) >> 3,
+        1.0,
+        0.0,
+    )
+    spread = jnp.where(
+        lax.broadcasted_iota(jnp.int32, (16, 128), 0)
+        == lax.broadcasted_iota(jnp.int32, (16, 128), 1) >> 3,
+        1.0,
+        0.0,
+    )
+    sums = jnp.dot(packed, group, precision=HIGHEST, preferred_element_type=F32)
     along = jnp.concatenate([gsum[4], gsum[5]], axis=0)
     left = jnp.where(((sub == 4) & (lane < 64)) | ((sub == 5) & (lane >= 64)), 1.0, 0.0)
     per_slot = lax.dot_general(
         left, along, (((1,), (1,)), ((), ())), precision=HIGHEST, preferred_element_type=F32
     )
-    sums = sums + jnp.dot(per_slot, spread[...], precision=HIGHEST, preferred_element_type=F32)
+    sums = sums + jnp.dot(per_slot, spread, precision=HIGHEST, preferred_element_type=F32)
     flag_rows = jnp.dot(
-        flags[...].astype(F32), spread[...], precision=HIGHEST, preferred_element_type=F32
+        flags[...].astype(F32), spread, precision=HIGHEST, preferred_element_type=F32
     )
     packed = jnp.zeros((16, 128), F32)
     sub16 = lax.broadcasted_iota(jnp.int32, (16, 128), 0)
@@ -349,6 +399,8 @@
         for i, row in enumerate((alpha, gain * (1.0 - alpha), gain, d_top, d_all)):
             packed = jnp.where(sub16 == 2 * i + h, row, packed)
     msg[...] = packed
+    for target, row in ((to_right, 160), (to_left, 160), (to_up, 80), (to_low, 80)):
+        target[pl.ds(row, 8), :] = packed[0:8]
 
 
 def conserved_node(state, cot, direction):
@@ -373,9 +425,89 @@
     )
 
 
-def kernel_faces(
-    ids, flow, cot, x_left, x_right, y_left, y_right, parts, zends, modes, msg, kxyt, kz, base, extra, slope, zacc, znext, zback
+def place(d, q):
+    return q if q in (0, 4) else 1 + PERMS[d][q - 1]
+
+
+def own_node(flow, cot, direction, rows):
+    return conserved_node(
+        [flow[q, rows, :] for q in range(5)], [cot[q, rows, :] for q in range(5)], direction
+    )
+
+
+def near_node(ref, count, start, direction):
+    return conserved_node(
+        [ref[pl.ds(q * count + start, 8), :] for q in range(5)],
+        [ref[pl.ds((5 + q) * count + start, 8), :] for q in range(5)],
+        direction,
+    )
+
+
+def kernel_local(
+    ids_hbm,
+    flow,
+    cot,
+    parts,
+    zends,
+    modes,
+    msg,
+    tables,
+    base,
+    extra,
+    slope,
+    zsum,
+    zacc,
+    znext,
+    zback,
+    ids,
+    sem,
 ):
+    copy = pltpu.make_async_copy(ids_hbm, ids, sem)
+    copy.start()
+
+    sub = lax.broadcasted_iota(jnp.int32, (8, 128), 0)
+    lane = lax.broadcasted_iota(jnp.int32, (8, 128), 1)
+    high = (sub >= 6) | ((lane & 7) >= 6)
+    tiles = []
+    for h in range(2):
+        d_top = msg[pl.ds(6 + h, 1), :]
+        d_all = msg[pl.ds(8 + h, 1), :]
+        both = d_top + d_all
+        mixed = jnp.where(high, both, d_all)
+        for x in range(8):
+            tiles.append(modes[pl.ds(h * 64 + 8 * x, 8), :] * (both if x >= 6 else mixed))
+    weighed = jnp.concatenate(tiles, axis=0)
+    weighed = jnp.dot(tables[2], weighed, precision=HIGHEST, preferred_element_type=F32)
+    weighed = jnp.dot(weighed, tables[3], precision=HIGHEST, preferred_element_type=F32)
+    for h in range(2):
+        for x in range(8):
+            rows = pl.ds(x * 16 + h * 8, 8)
+            density = flow[0, rows, :]
+            inv = rcp(density)
+            vel = [flow[1 + i, rows, :] * inv for i in range(3)]
+            square = vel[0] * vel[0] + vel[1] * vel[1] + vel[2] * vel[2]
+            pres = 0.4 * (flow[4, rows, :] - 0.5 * density * square)
+            value = weighed[h * 64 + 8 * x : h * 64 + 8 * x + 8]
+            pull_e = 0.4 * (value * density)
+            slope[0, rows, :] = value * pres + (0.5 * pull_e) * square
+            for i in range(3):
+                slope[1 + i, rows, :] = -(pull_e * vel[i])
+            slope[4, rows, :] = pull_e
+
+    copy.wait()
+    row = lax.broadcasted_iota(jnp.int32, (128, 128), 0)
+    lanes = lax.broadcasted_iota(jnp.int32, (8, 128), 1)
+    above = jnp.zeros((8, 128), jnp.int32)
+    for k in range(16):
+        above = jnp.where((lanes >> 3) == k, ids[k], above)
+    above = above * 8 + (lanes & 7)
+    above = jnp.concatenate([above] * 16, axis=0)
+    up = jnp.where(above == row, 1.0, 0.0)
+    own = msg[0:8, :]
+    zsum[...] = jnp.dot(own, up, precision=HIGHEST, preferred_element_type=F32) + lax.dot_general(
+        own, up, (((1,), (1,)), ((), ())), precision=HIGHEST, preferred_element_type=F32
+    )
+
     for k in range(16):
         znext[:, pl.ds(k, 1), :] = zends[:, pl.ds(ids[k], 1), :]
     for h in range(2):
@@ -391,9 +523,6 @@
             zback[5 + q, pl.ds(h * 8, 8), :] = up_g[q]
     for k in range(16):
         zacc[:, pl.ds(16 + ids[k], 1), :] = zback[:, pl.ds(k, 1), :]
-
-    def place(d, q):
-        return q if q in (0, 4) else 1 + PERMS[d][q - 1]
 
     back = [[place(d, q) for q in range(5)] for d in range(3)]
     for group_at, target, offset in ((0, base, 0), (1, extra, 0), (2, base, 5), (3, extra, 5)):
@@ -424,83 +553,45 @@
                     )
                     target[offset + q, pl.ds(x * 16 + h * 8, 8), :] = value
 
-    def own(direction, rows):
-        return conserved_node([flow[q, rows, :] for q in range(5)], [cot[q, rows, :] for q in range(5)], direction)
-
-    def add(direction, rows, res, grad):
+    rows = [pl.ds(7, 8, stride=16), pl.ds(8, 8, stride=16)]
+    shares = face_shares(own_node(flow, cot, 1, rows[0]), own_node(flow, cot, 1, rows[1]))
+    for side in range(2):
         for q in range(5):
-            p = place(direction, q)
-            base[p, rows, :] += res[q]
-            base[5 + p, rows, :] += grad[q]
-
-    def near(ref, rows, direction):
-        return conserved_node([ref[q, rows, :] for q in range(5)], [ref[5 + q, rows, :] for q in range(5)], direction)
-
+            p = place(1, q)
+            base[p, rows[side], :] += shares[2 * side][q]
+            base[5 + p, rows[side], :] += shares[2 * side + 1][q]
+
+
+def kernel_blend(
+    msg,
+    zsum,
+    from_left,
+    from_right,
+    from_low,
+    from_up,
+    flow,
+    cot,
+    base,
+    extra,
+    slope,
+    residual_hbm,
+    grad_hbm,
+    total,
+    sems,
+):
     for h in range(2):
-        here = pl.ds(h * 8, 8)
-        top = pl.ds(112 + h * 8, 8)
-        low_r, low_g, up_r, up_g = face_shares(near(x_left, here, 0), own(0, here))
-        add(0, here, up_r, up_g)
-        low_r, low_g, up_r, up_g = face_shares(own(0, top), near(x_right, here, 0))
-        add(0, top, low_r, low_g)
-    whole = pl.ds(0, 8)
-    rows = [pl.ds(k, 8, stride=16) for k in (0, 7, 8, 15)]
-    low_r, low_g, up_r, up_g = face_shares(near(y_left, whole, 1), own(1, rows[0]))
-    add(1, rows[0], up_r, up_g)
-    low_r, low_g, up_r, up_g = face_shares(own(1, rows[1]), own(1, rows[2]))
-    add(1, rows[1], low_r, low_g)
-    add(1, rows[2], up_r, up_g)
-    low_r, low_g, up_r, up_g = face_shares(own(1, rows[3]), near(y_right, whole, 1))
-    add(1, rows[3], low_r, low_g)
-
-    sub = lax.broadcasted_iota(jnp.int32, (8, 128), 0)
-    lane = lax.broadcasted_iota(jnp.int32, (8, 128), 1)
-    high = (sub >= 6) | ((lane & 7) >= 6)
-    tiles = []
-    for h in range(2):
-        d_top = msg[pl.ds(6 + h, 1), :]
-        d_all = msg[pl.ds(8 + h, 1), :]
-        both = d_top + d_all
-        mixed = jnp.where(high, both, d_all)
-        for x in range(8):
-            tiles.append(modes[pl.ds(h * 64 + 8 * x, 8), :] * (both if x >= 6 else mixed))
-    weighed = jnp.concatenate(tiles, axis=0)
-    weighed = jnp.dot(kxyt[...], weighed, precision=HIGHEST, preferred_element_type=F32)
-    weighed = jnp.dot(weighed, kz[...], precision=HIGHEST, preferred_element_type=F32)
-    for h in range(2):
-        for x in range(8):
-            rows = pl.ds(x * 16 + h * 8, 8)
-            density = flow[0, rows, :]
-            inv = rcp(density)
-            vel = [flow[1 + i, rows, :] * inv for i in range(3)]
-            square = vel[0] * vel[0] + vel[1] * vel[1] + vel[2] * vel[2]
-            pres = 0.4 * (flow[4, rows, :] - 0.5 * density * square)
-            value = weighed[h * 64 + 8 * x : h * 64 + 8 * x + 8]
-            pull_e = 0.4 * (value * density)
-            slope[0, rows, :] = value * pres + (0.5 * pull_e) * square
-            for i in range(3):
-                slope[1 + i, rows, :] = -(pull_e * vel[i])
-            slope[4, rows, :] = pull_e
-
-
-def kernel_blend(ids, msg, from_left, from_right, from_low, from_up, base, extra, slope, residual, grad):
-    row = lax.broadcasted_iota(jnp.int32, (128, 128), 0)
-    lane = lax.broadcasted_iota(jnp.int32, (128, 128), 1)
-    slot = lane >> 3
-    above = jnp.zeros((128, 128), jnp.int32)
-    for k in range(16):
-        above = jnp.where(slot == k, ids[k], above)
-    up = jnp.where((above * 8 + (lane & 7)) == row, 1.0, 0.0)
-    own = msg[0:8, :]
-    beside = jnp.dot(own, up, precision=HIGHEST, preferred_element_type=F32) + lax.dot_general(
-        own, up, (((1,), (1,)), ((), ())), precision=HIGHEST, preferred_element_type=F32
-    )
-    beside = beside + from_left[0:8, :] + from_right[0:8, :]
-    for h in range(2):
+
         def beside_of(i):
-            low = from_low[2 * i + 1 : 2 * i + 2, :] if h == 0 else msg[2 * i : 2 * i + 1, :]
-            high = msg[2 * i + 1 : 2 * i + 2, :] if h == 0 else from_up[2 * i : 2 * i + 1, :]
-            return beside[2 * i + h : 2 * i + h + 1, :] + low + high
+            r = 2 * i + h
+            low = from_low[81 + 2 * i : 82 + 2 * i, :] if h == 0 else msg[2 * i : 2 * i + 1, :]
+            high = msg[2 * i + 1 : 2 * i + 2, :] if h == 0 else from_up[80 + 2 * i : 81 + 2 * i, :]
+            return (
+                zsum[r : r + 1, :]
+                + from_left[160 + r : 161 + r, :]
+                + from_right[160 + r : 161 + r, :]
+                + low
+                + high
+            )
 
         alpha = msg[h : h + 1, :]
         gain = msg[4 + h : 5 + h, :]
@@ -512,10 +603,36 @@
         for x in range(8):
             rows = pl.ds(x * 16 + h * 8, 8)
             for q in range(5):
-                residual[q, rows, :] = base[q, rows, :] + smooth * extra[q, rows, :]
-                grad[q, rows, :] = (
+                total[q, rows, :] = base[q, rows, :] + smooth * extra[q, rows, :]
+                total[5 + q, rows, :] = (
                     base[5 + q, rows, :] + smooth * extra[5 + q, rows, :] + pull * slope[q, rows, :]
                 )
+
+    def add(direction, rows, res, grad):
+        for q in range(5):
+            p = place(direction, q)
+            total[p, rows, :] += res[q]
+            total[5 + p, rows, :] += grad[q]
+
+    for h in range(2):
+        here, top = pl.ds(h * 8, 8), pl.ds(112 + h * 8, 8)
+        shares = face_shares(near_node(from_left, 16, h * 8, 0), own_node(flow, cot, 0, here))
+        add(0, here, shares[2], shares[3])
+        shares = face_shares(own_node(flow, cot, 0, top), near_node(from_right, 16, h * 8, 0))
+        add(0, top, shares[0], shares[1])
+    here, top = pl.ds(0, 8, stride=16), pl.ds(15, 8, stride=16)
+    shares = face_shares(near_node(from_low, 8, 0, 1), own_node(flow, cot, 1, here))
+    add(1, here, shares[2], shares[3])
+    shares = face_shares(own_node(flow, cot, 1, top), near_node(from_up, 8, 0, 1))
+    add(1, top, shares[0], shares[1])
+    copies = [
+        pltpu.make_async_copy(total.at[pl.ds(0, 5)], residual_hbm, sems.at[0]),
+        pltpu.make_async_copy(total.at[pl.ds(5, 5)], grad_hbm, sems.at[1]),
+    ]
+    for copy in copies:
+        copy.start()
+    for copy in copies:
+        copy.wait()
 
 
 def shifted(value, axis, steps):
@@ -525,74 +642,82 @@
 
 def shape(*dims):
     return jax.ShapeDtypeStruct(dims, F32)
+
+
+def in_hbm(value):
+    return pltpu.with_memory_space_constraint(value, pltpu.HBM)
 
 
 def shards(flow_state, cotangent, clip_flags, successor_ids):
     flow = flow_state.reshape(5, ROWS, 128)
     cot = cotangent.reshape(5, ROWS, 128)
     vmem = pl.BlockSpec(memory_space=pltpu.VMEM)
-    smem = pl.BlockSpec(memory_space=pltpu.SMEM)
-    params = pltpu.CompilerParams(vmem_limit_bytes=48 * 1024 * 1024)
-
-    both = jnp.concatenate([flow_state, cotangent], axis=0)
-    x_left = shifted(both[:, 7], "gx", 1)
-    x_right = shifted(both[:, 0], "gx", -1)
-    y_left = shifted(both[:, :, 15], "gy", 1)
-    y_right = shifted(both[:, :, 0], "gy", -1)
-
+    hbm = pl.BlockSpec(memory_space=pltpu.HBM)
     modal = np.asarray(TO_MODAL, np.float32)
     kxy = np.kron(np.eye(2), np.kron(modal, modal)).astype(np.float32)
     kz = np.kron(np.eye(16), modal).astype(np.float32)
-    group = np.kron(np.eye(16), np.ones((8, 8))).astype(np.float32)
-    spread = np.kron(np.eye(16), np.ones((1, 8))).astype(np.float32)
-
-    parts, zends, modes, msg = pl.pallas_call(
+    constants = np.stack([kxy, kz.T, kxy.T, kz])
+
+    parts, zends, modes, msg, to_right, to_left, to_up, to_low, flow_v, cot_v, tables = pl.pallas_call(
         kernel_volume,
-        out_shape=(shape(3, 20, ROWS, 128), shape(NQ, 32, 128), shape(ROWS, 128), shape(16, 128)),
-        in_specs=[vmem] * 7,
-        out_specs=[vmem] * 4,
+        out_shape=(
+            shape(3, 20, ROWS, 128),
+            shape(NQ, 32, 128),
+            shape(ROWS, 128),
+            shape(16, 128),
+            shape(168, 128),
+            shape(168, 128),
+            shape(88, 128),
+            shape(88, 128),
+            shape(5, ROWS, 128),
+            shape(5, ROWS, 128),
+            shape(4, 128, 128),
+        ),
+        in_specs=[hbm] * 4,
+        out_specs=[vmem] * 11,
         scratch_shapes=[
             pltpu.VMEM((NQ, ROWS, 128), F32),
             pltpu.VMEM((NQ, ROWS, 128), F32),
             pltpu.VMEM((3, NQ, ROWS, 128), F32),
             pltpu.VMEM((ROWS, 128), F32),
             pltpu.VMEM((6, 8, 128), F32),
+            pltpu.VMEM((2, 16), jnp.int32),
+            pltpu.SemaphoreType.DMA((4,)),
         ],
-        compiler_params=params,
+        compiler_params=pltpu.CompilerParams(vmem_limit_bytes=20 * 1024 * 1024),
         name="volume",
-    )(flow, cot, clip_flags.reshape(2, 16), kxy, np.ascontiguousarray(kz.T), group, spread)
-
-    sent = msg[0:8]
-    from_left = shifted(sent, "gx", 1)
-    from_right = shifted(sent, "gx", -1)
-    from_low = shifted(sent, "gy", 1)
-    from_up = shifted(sent, "gy", -1)
-
-    base, extra, slope = pl.pallas_call(
-        kernel_faces,
-        out_shape=(shape(10, ROWS, 128), shape(10, ROWS, 128), shape(5, ROWS, 128)),
-        in_specs=[smem] + [vmem] * 12,
-        out_specs=[vmem] * 3,
+    )(in_hbm(flow), in_hbm(cot), in_hbm(clip_flags.reshape(2, 16)), in_hbm(jnp.asarray(constants)))
+
+    from_low = shifted(to_up, "gy", 1)
+    from_up = shifted(to_low, "gy", -1)
+    from_left = shifted(to_right, "gx", 1)
+    from_right = shifted(to_left, "gx", -1)
+
+    base, extra, slope, zsum = pl.pallas_call(
+        kernel_local,
+        out_shape=(shape(10, ROWS, 128), shape(10, ROWS, 128), shape(5, ROWS, 128), shape(8, 128)),
+        in_specs=[hbm] + [vmem] * 7,
+        out_specs=[vmem] * 4,
         scratch_shapes=[
             pltpu.VMEM((10, 32, 128), F32),
             pltpu.VMEM((NQ, 16, 128), F32),
             pltpu.VMEM((10, 16, 128), F32),
+            pltpu.SMEM((16,), jnp.int32),
+            pltpu.SemaphoreType.DMA(()),
         ],
-        compiler_params=params,
-        name="faces",
-    )(
-        successor_ids, flow, cot, x_left, x_right, y_left, y_right, parts, zends, modes, msg,
-        np.ascontiguousarray(kxy.T), kz,
-    )
+        compiler_params=pltpu.CompilerParams(vmem_limit_bytes=16 * 1024 * 1024),
+        name="local",
+    )(in_hbm(successor_ids), flow_v, cot_v, parts, zends, modes, msg, tables)
 
     residual, grad = pl.pallas_call(
         kernel_blend,
         out_shape=(shape(5, ROWS, 128), shape(5, ROWS, 128)),
-        in_specs=[smem] + [vmem] * 8,
-        out_specs=[vmem] * 2,
-        compiler_params=params,
+        in_specs=[vmem] * 11,
+        out_specs=[hbm] * 2,
+        scratch_shapes=[pltpu.VMEM((10, ROWS, 128), F32), pltpu.SemaphoreType.DMA((2,))],
+        compiler_params=pltpu.CompilerParams(vmem_limit_bytes=16 * 1024 * 1024),
         name="blend",
-    )(successor_ids, msg, from_left, from_right, from_low, from_up, base, extra, slope)
+    )(msg, zsum, from_left, from_right, from_low, from_up, flow_v, cot_v, base, extra, slope)
     return residual.reshape(flow_state.shape), grad.reshape(flow_state.shape)
 
 

time: 42.8 us -> 26.1 us (0.61)
  the two profiles are of different devices: /device:TPU:1 before, /device:TPU:64 now
where the time goes in v1:
time: 26.1 us; the launch traced here: 26 us
  starting transfers between devices  10.5 us (40%)
  Pallas kernels  10.3 us (39%)
  waiting for transfers between devices  4.48 us (17%)
  between operations  0.66 us (3%)
    ppermute x4, starting transfers between devices, shifted(): lax.ppermute(value, axis, [(i, (i + steps) % count) for i in range(count)])  10.5 us
    pallas_call x1, Pallas kernels, shards(): pl.pallas_call(kernel_volume, out_shape=(shape(3, 20, ROWS, 128), shape(N...  7.44 us
    ppermute x4, waiting for transfers between devices, shifted(): lax.ppermute(value, axis, [(i, (i + steps) % count) for i in range(count)])  4.48 us
    pallas_call x1, Pallas kernels, shards(): pl.pallas_call(kernel_local, out_shape=(shape(10, ROWS, 128), shape(10, R...  1.68 us
    pallas_call x1, Pallas kernels, shards(): pl.pallas_call(kernel_blend, out_shape=(shape(5, ROWS, 128), shape(5, ROW...  1.22 us
  transfers between devices with their start and end apart: 4, of which 1 were waited for; matrix products, arithmetic and copies ran while one was open for 0% of the time, Pallas kernels for 6%

profile of v1, /device:TPU:64, one launch (start us, length us, event | category | flops | bytes accessed | tf_op | source)
XLA Modules:
  0.0 26.0 jit_solution(17001940420149632367)
XLA Ops:
  0.6 7.4 %volume.1 = (f32[3,20,128,128]{3,2,1,0:T(8,128)S(1)}, f32[13,32,128]{2,1,0:T(8,128)S(1)}, f32[128,128]{1,0:T(8,128)S(1)}, f32[16,128]{1,0:T(8,128)S(1)}, f32[168...) custom-call(f32[5,128,128]{2,1,0:T(8,128)} %bitcast.5, ...), custom_call_target="tpu_custom_call" | custom-call | tf_op jit(solution)/shard_map/volume/pallas_call | solution.py:661
  8.1 0.1 collective-permute-start
  8.2 6.1 %collective-permute-start.1 = (f32[168,128]{1,0:T(8,128)S(1)}, f32[168,128]{1,0:T(8,128)S(1)}, u32[]{:S(2)}, u32[]{:S(2)}) collective-permute-start(f32[168,128]{1,0:T(8,128)S(1)} %get-tuple-element.28), channel_id=1, source_target_pairs={{0,252},{4,0},{8,4},{12,8},{16,12},{20,16},{24,20},{28,24},{32,28}... | collective-permute-start | bytes 258056 | tf_op jit(solution)/shard_map/ppermute | solution.py:640
  14.2 4.4 %collective-permute-start.2 = (f32[88,128]{1,0:T(8,128)S(1)}, f32[88,128]{1,0:T(8,128)S(1)}, u32[]{:S(2)}, u32[]{:S(2)}) collective-permute-start(f32[88,128]{1,0:T(8,128)S(1)} %get-tuple-element.29), channel_id=1, source_target_pairs={{0,1},{1,2},{2,3},{3,0},{4,5},{5,6},{6,7},{7,4},{8,9},{9,10},{10,1... | collective-permute-start | bytes 135176 | tf_op jit(solution)/shard_map/ppermute | solution.py:640
  18.6 0.0 collective-permute-start.3
  18.6 1.7 %local.1 = (f32[10,128,128]{2,1,0:T(8,128)S(1)}, f32[10,128,128]{2,1,0:T(8,128)S(1)}, f32[5,128,128]{2,1,0:T(8,128)S(1)}, f32[8,128]{1,0:T(8,128)S(1)}) custom-call(s32[16]{0:T(128)} %ids_hbm.1, f32[5,128,128]{2,1,0:T(8,128)S(1)} %get-tuple-element.20.flow, f32[5,128,128]{2,1,0:T(8,128)S(1)} %get-tuple-element.21.cot, ...), custom_call_target="tpu_custom_call" | custom-call | tf_op jit(solution)/shard_map/local/pallas_call | solution.py:696
  20.3 0.0 collective-permute-done.2.from_low
  20.3 4.5 %collective-permute-done.3.from_up = f32[88,128]{1,0:T(8,128)S(1)} collective-permute-done((f32[88,128]{1,0:T(8,128)S(1)}, f32[88,128]{1,0:T(8,128)S(1)}, u32[]{:S(2)}, u32[]{:S(2)}) %collective-permute-start.3) | collective-permute-done | bytes 45088 | tf_op jit(solution)/shard_map/ppermute | solution.py:640
  24.8 0.0 collective-permute-done.from_left
  24.8 0.0 collective-permute-done.1.from_right
  24.8 1.2 %blend.1 = (f32[5,128,128]{2,1,0:T(8,128)}, f32[5,128,128]{2,1,0:T(8,128)}) custom-call(f32[16,128]{1,0:T(8,128)S(1)} %get-tuple-element.19.msg, f32[8,128]{1,0:T(8,128)S(1)} %get-tuple-element.26.zsum, f32[168,128]{1,0:T(8,128)S(1)} %collective-permute-done.from_left, f32[168,128]{1,0:T(8,128)S(1)} %collective-permute-done.1.from_right, ...), custom_call_target="tpu_custom_call" | custom-call | tf_op jit(solution)/shard_map/blend/pallas_call | solution.py:712
Async XLA Ops:
  8.1 16.7 %collective-permute-start = (f32[168,128]{1,0:T(8,128)S(1)}, f32[168,128]{1,0:T(8,128)S(1)}, u32[]{:S(2)}, u32[]{:S(2)}) collective-permute-start(f32[168,128]{1,0:T(8,128)S(1)} %get-tuple-element.27), channel_id=1, source_target_pairs={{0,4},{4,8},{8,12},{12,16},{16,20},{20,24},{24,28},{28,32},{32,36}... | collective-permute-start | bytes 258056 | tf_op jit(solution)/shard_map/ppermute | solution.py:640
  8.2 16.6 %collective-permute-start.1 = (f32[168,128]{1,0:T(8,128)S(1)}, f32[168,128]{1,0:T(8,128)S(1)}, u32[]{:S(2)}, u32[]{:S(2)}) collective-permute-start(f32[168,128]{1,0:T(8,128)S(1)} %get-tuple-element.28), channel_id=1, source_target_pairs={{0,252},{4,0},{8,4},{12,8},{16,12},{20,16},{24,20},{28,24},{32,28}... | collective-permute-start | bytes 258056 | tf_op jit(solution)/shard_map/ppermute | solution.py:640
  14.2 6.1 %collective-permute-start.2 = (f32[88,128]{1,0:T(8,128)S(1)}, f32[88,128]{1,0:T(8,128)S(1)}, u32[]{:S(2)}, u32[]{:S(2)}) collective-permute-start(f32[88,128]{1,0:T(8,128)S(1)} %get-tuple-element.29), channel_id=1, source_target_pairs={{0,1},{1,2},{2,3},{3,0},{4,5},{5,6},{6,7},{7,4},{8,9},{9,10},{10,1... | collective-permute-start | bytes 135176 | tf_op jit(solution)/shard_map/ppermute | solution.py:640
  18.6 6.2 %collective-permute-start.3 = (f32[88,128]{1,0:T(8,128)S(1)}, f32[88,128]{1,0:T(8,128)S(1)}, u32[]{:S(2)}, u32[]{:S(2)}) collective-permute-start(f32[88,128]{1,0:T(8,128)S(1)} %get-tuple-element.30), channel_id=1, source_target_pairs={{0,3},{1,0},{2,1},{3,2},{4,7},{5,4},{6,5},{7,6},{8,11},{9,8},{10,9... | collective-permute-start | bytes 135176 | tf_op jit(solution)/shard_map/ppermute | solution.py:640

commit v2 on v1

--- a/solution.py
+++ b/solution.py
@@ -73,6 +73,8 @@
     return np.where(square < 1e-2, series, exact)
 
 
+PAIR = {pair: i for i, pair in enumerate((k, j) for k in range(7) for j in range(k + 1, 8))}
+
 MEAN_R = fitted(sinhc, 3.0, 4)
 SLOPE_R = fitted(sinhc_slope, 3.0, 3)
 MEAN_B = fitted(sinhc, 12.0, 5)
@@ -150,25 +152,30 @@
     return flux, weight, direct, -0.25 * dot
 
 
-def kernel_volume(
+def lane_tables():
+    sub = lax.broadcasted_iota(jnp.int32, (8, 128), 0)
+    lane = lax.broadcasted_iota(jnp.int32, (8, 128), 1)
+    return sub, lane, (sub >= 6) | ((lane & 7) >= 6)
+
+
+def kernel_first(
     flow_hbm,
     cot_hbm,
     flags_hbm,
     tables_hbm,
-    out,
-    zends,
+    lines,
+    mid,
     modes,
     msg,
-    to_right,
-    to_left,
-    to_up,
-    to_low,
+    to_partner,
+    to_other,
+    to_ahead,
+    to_behind,
     flow,
     cot,
     tables,
     nat,
     turned,
-    lines,
     prod,
     gsum,
     flags,
@@ -182,14 +189,18 @@
     ]
     for copy in copies:
         copy.start()
+    even_x = lax.axis_index("gx") % 2 == 0
+    even_y = lax.axis_index("gy") % 2 == 0
     copies[0].wait()
     copies[1].wait()
     for c in range(10):
         source, q = (flow, c) if c < 5 else (cot, c - 5)
-        to_right[pl.ds(16 * c, 16), :] = source[q, pl.ds(112, 16), :]
-        to_left[pl.ds(16 * c, 16), :] = source[q, pl.ds(0, 16), :]
-        to_up[pl.ds(8 * c, 8), :] = source[q, pl.ds(15, 8, stride=16), :]
-        to_low[pl.ds(8 * c, 8), :] = source[q, pl.ds(0, 8, stride=16), :]
+        top, low = source[q, pl.ds(112, 16), :], source[q, pl.ds(0, 16), :]
+        to_partner[pl.ds(16 * c, 16), :] = jnp.where(even_x, top, low)
+        to_other[pl.ds(16 * c, 16), :] = jnp.where(even_x, low, top)
+        top, low = source[q, pl.ds(15, 8, stride=16), :], source[q, pl.ds(0, 8, stride=16), :]
+        to_ahead[pl.ds(8 * c, 8), :] = jnp.where(even_y, top, low)
+        to_behind[pl.ds(8 * c, 8), :] = jnp.where(even_y, low, top)
 
     for x in range(8):
         for h in range(2):
@@ -220,187 +231,110 @@
                     rows = pl.ds(h * 64 + 8 * k, 8) if d == 0 else pl.ds(h * 64 + k, 8, stride=8)
                     value = source[order[q], rows, :]
                     lines[d, q, pl.ds(h * 64 + 8 * k, 8), :] = value * INV_W[k] if q >= 8 else value
-    for q in range(NQ):
-        for end in range(2):
-            for h in range(2):
-                zends[q, pl.ds(end * 16 + h * 8, 8), :] = lines[2, q, pl.ds(h * 64 + 56 * end, 8), :]
-
-    def one(step, carry):
-        d = step // 2
-        base = (step % 2) * 64
-
-        def rows(k):
-            return pl.ds(pl.multiple_of(base + 8 * k, 8), 8)
-
-        for k in range(7):
-            a = [lines[d, q, rows(k), :] for q in range(NQ)]
-            acc = [None] * 11 if k == 0 else [out[d, q, rows(k), :] for q in range(11)]
-            for j in range(k + 1, 8):
-                skew = float(SKEW[k, j])
-                b = [lines[d, q, rows(j), :] for q in range(NQ)]
-                vn, v1, v2 = (a[i] + b[i] for i in range(3))
-                delta = [a[8 + i] - b[8 + i] for i in range(5)]
-                y = a[5] - b[5]
-                square = y * y
-                scale = (0.25 * skew) * (a[4] * b[4])
-                mean = scale * horner(MEAN_R, square)
-                slope = (scale * y) * horner(SLOPE_R, square)
-                yb = a[7] - b[7]
-                square_b = yb * yb
-                quot = rcp(horner(MEAN_B, square_b))
-                inv5 = (a[6] * b[6]) * quot
-                tilt = yb * (horner(SLOPE_B, square_b) * quot)
-                dot = a[0] * b[0] + a[1] * b[1] + a[2] * b[2] + inv5
-                mass = mean * vn
-                half = 0.5 * skew
-                flux = [
-                    mass,
-                    mass * vn + half * (a[3] + b[3]),
-                    mass * v1,
-                    mass * v2,
-                    mass * dot + half * (a[3] * b[0] + b[3] * a[0]),
-                ]
-                phi = delta[0] + delta[1] * vn + delta[2] * v1 + delta[3] * v2 + delta[4] * dot
-                common = phi * mean + delta[1] * mass
-                t = half * delta[4]
-                u = half * delta[1]
-                w = mass * delta[4]
-                r1 = mass * delta[2]
-                r2 = mass * delta[3]
-                pp = phi * mass
-                qq = (phi * vn) * slope
-                xx = w * inv5
-                zz = xx * tilt
-                grad_a = [
-                    pp + qq,
-                    common + w * b[0] + t * b[3],
-                    r1 + w * b[1],
-                    r2 + w * b[2],
-                    u + t * b[0],
-                    xx + zz,
-                ]
-                grad_b = [
-                    pp - qq,
-                    common + w * a[0] + t * a[3],
-                    r1 + w * a[1],
-                    r2 + w * a[2],
-                    u + t * a[0],
-                    xx - zz,
-                ]
-                for q in range(5):
-                    acc[q] = flux[q] if acc[q] is None else acc[q] + flux[q]
-                    before = 0.0 if k == 0 else out[d, q, rows(j), :]
-                    out[d, q, rows(j), :] = before - flux[q]
-                for q in range(6):
-                    acc[5 + q] = grad_a[q] if acc[5 + q] is None else acc[5 + q] + grad_a[q]
-                    out[d, 5 + q, rows(j), :] = grad_b[q] if k == 0 else out[d, 5 + q, rows(j), :] + grad_b[q]
-            for q in range(11):
-                out[d, q, rows(k), :] = acc[q]
-
-        low = None
-        zero = jnp.zeros((8, 128), F32)
-        low_flux, low_weight, low_direct, low_dot = [zero] * 5, [zero] * 5, [zero] * 5, zero
-        gained = zero
-        for k in range(9):
-            if k < 8:
-                a = [lines[d, q, rows(k), :] for q in range(NQ)]
-                node = Node(a[0:3], a[3], a[4], a[6], [0.5 * a[8]] + a[9:13])
-            if k == 0:
-                low = node
-                continue
-            if k < 8:
-                flux, weight, direct, dot = face(low, node)
-            else:
-                flux, weight, direct, dot = [zero] * 5, [zero] * 5, [zero] * 5, zero
-            m = k - 1
-            total = [out[d, q, rows(m), :] for q in range(11)]
-            total[0] = 2.0 * total[0]
-            for q in range(5):
-                diff = total[q] - (flux[q] - low_flux[q])
-                gained = gained + low.cot[q] * diff
-                out[d, q, rows(m), :] = total[q] * (-INV_W[m])
-                out[d, 5 + q, rows(m), :] = diff * INV_W[m]
-            fv = low.pull(
-                [0.5 * (x + z) for x, z in zip(low_weight, weight)],
-                [x - z for x, z in zip(direct, low_direct)],
-                low_dot + dot,
-            )
-            inv = rcp(low.state[0])
-            beta = 0.5 * total[10]
-            g_rho = (beta - 0.5 * total[5]) * inv
-            g_e = -0.4 * (total[9] + beta * rcp(low.pres))
-            g_m = [-(total[6 + i] * inv) - g_e * low.vel[i] for i in range(3)]
-            inner = g_m[0] * low.vel[0] + g_m[1] * low.vel[1] + g_m[2] * low.vel[2]
-            dg = [g_rho - inner - (0.5 * g_e) * low.square] + g_m + [g_e]
-            for q in range(5):
-                out[d, 10 + q, rows(m), :] = dg[q]
-                out[d, 15 + q, rows(m), :] = fv[q] - dg[q]
-            low, low_flux, low_weight, low_direct, low_dot = node, flux, weight, direct, dot
-        gsum[step] = gained
-        return carry
-
-    lax.fori_loop(0, 6, one, 0)
 
     copies[2].wait()
     copies[3].wait()
+    sub, lane, high = lane_tables()
     coeffs = jnp.dot(tables[0], prod[...], precision=HIGHEST, preferred_element_type=F32)
     coeffs = jnp.dot(coeffs, tables[1], precision=HIGHEST, preferred_element_type=F32)
     modes[...] = coeffs
     squares = coeffs * coeffs
-    sub = lax.broadcasted_iota(jnp.int32, (8, 128), 0)
-    lane = lax.broadcasted_iota(jnp.int32, (8, 128), 1)
-    high = (sub >= 6) | ((lane & 7) >= 6)
-    packed = jnp.zeros((8, 128), F32)
-    tops, alls, gains = [], [], []
-    for h in range(2):
-        every = squares[h * 64 : h * 64 + 8]
-        for x in range(1, 6):
-            every = every + squares[h * 64 + 8 * x : h * 64 + 8 * x + 8]
-        ends = squares[h * 64 + 48 : h * 64 + 56] + squares[h * 64 + 56 : h * 64 + 64]
-        tops.append(jnp.sum(jnp.where(high, every, 0.0) + ends, axis=0, keepdims=True))
-        alls.append(jnp.sum(every + ends, axis=0, keepdims=True))
-        gains.append(jnp.sum(gsum[h] + gsum[2 + h], axis=0, keepdims=True))
-    for i, row in enumerate(tops + alls + gains):
-        packed = jnp.where(sub == i, row, packed)
     group = jnp.where(
         lax.broadcasted_iota(jnp.int32, (128, 128), 0) >> 3
         == lax.broadcasted_iota(jnp.int32, (128, 128), 1) >> 3,
         1.0,
         0.0,
     )
-    spread = jnp.where(
+    spread = (
         lax.broadcasted_iota(jnp.int32, (16, 128), 0)
-        == lax.broadcasted_iota(jnp.int32, (16, 128), 1) >> 3,
-        1.0,
-        0.0,
+        == lax.broadcasted_iota(jnp.int32, (16, 128), 1) >> 3
     )
+    packed = jnp.zeros((8, 128), F32)
+    for h in range(2):
+        every = squares[h * 64 : h * 64 + 8]
+        for x in range(1, 6):
+            every = every + squares[h * 64 + 8 * x : h * 64 + 8 * x + 8]
+        ends = squares[h * 64 + 48 : h * 64 + 56] + squares[h * 64 + 56 : h * 64 + 64]
+        top = jnp.sum(jnp.where(high, every, 0.0) + ends, axis=0, keepdims=True)
+        packed = jnp.where(sub == h, top, packed)
+        packed = jnp.where(sub == 2 + h, jnp.sum(every + ends, axis=0, keepdims=True), packed)
     sums = jnp.dot(packed, group, precision=HIGHEST, preferred_element_type=F32)
-    along = jnp.concatenate([gsum[4], gsum[5]], axis=0)
-    left = jnp.where(((sub == 4) & (lane < 64)) | ((sub == 5) & (lane >= 64)), 1.0, 0.0)
-    per_slot = lax.dot_general(
-        left, along, (((1,), (1,)), ((), ())), precision=HIGHEST, preferred_element_type=F32
+    flag_rows = jnp.dot(
+        flags[...].astype(F32),
+        jnp.where(spread, 1.0, 0.0),
+        precision=HIGHEST,
+        preferred_element_type=F32,
     )
-    sums = sums + jnp.dot(per_slot, spread, precision=HIGHEST, preferred_element_type=F32)
-    flag_rows = jnp.dot(
-        flags[...].astype(F32), spread, precision=HIGHEST, preferred_element_type=F32
-    )
-    packed = jnp.zeros((16, 128), F32)
     sub16 = lax.broadcasted_iota(jnp.int32, (16, 128), 0)
+    factors = jnp.zeros((16, 128), F32)
     for h in range(2):
         top = sums[h : h + 1] + EPS
         every = 0.01 * (sums[2 + h : 3 + h] + EPS)
-        gain = sums[4 + h : 5 + h]
         flag = flag_rows[h : h + 1]
         over = rcp(top + every)
         keep = flag < 0.5
         alpha = jnp.where(keep, 0.5 * top * over, jnp.where(flag > 1.5, 0.5, 0.0))
         d_top = jnp.where(keep, every * over * over, 0.0)
         d_all = jnp.where(keep, -0.01 * top * over * over, 0.0)
-        for i, row in enumerate((alpha, gain * (1.0 - alpha), gain, d_top, d_all)):
-            packed = jnp.where(sub16 == 2 * i + h, row, packed)
-    msg[...] = packed
-    for target, row in ((to_right, 160), (to_left, 160), (to_up, 80), (to_low, 80)):
-        target[pl.ds(row, 8), :] = packed[0:8]
+        for i, row in ((0, alpha), (6, d_top), (8, d_all)):
+            factors = jnp.where(sub16 == i + h, row, factors)
+    msg[...] = factors
+
+    def one(step, carry):
+        d = step // 2
+        base = (step % 2) * 64
+
+        def load(k):
+            rows = pl.ds(pl.multiple_of(base + 8 * k, 8), 8)
+            return [lines[d, q, rows, :] for q in range(NQ)]
+
+        gained = jnp.zeros((8, 128), F32)
+        for k in range(7):
+            a = load(k)
+            for j in range(k + 1, 8):
+                skew = float(SKEW[k, j])
+                b = load(j)
+                vn, v1, v2 = (a[i] + b[i] for i in range(3))
+                delta = [a[8 + i] - b[8 + i] for i in range(5)]
+                y = a[5] - b[5]
+                mean = ((0.25 * skew) * (a[4] * b[4])) * horner(MEAN_R, y * y)
+                yb = a[7] - b[7]
+                quot = rcp(horner(MEAN_B, yb * yb))
+                inv5 = (a[6] * b[6]) * quot
+                dot = a[0] * b[0] + a[1] * b[1] + a[2] * b[2] + inv5
+                phi = delta[0] + delta[1] * vn + delta[2] * v1 + delta[3] * v2 + delta[4] * dot
+                for q, value in enumerate((mean, quot, inv5, dot, phi)):
+                    mid[step, 5 * PAIR[k, j] + q] = value
+                work = delta[1] * (a[3] + b[3]) + delta[4] * (a[3] * b[0] + b[3] * a[0])
+                gained = gained + (mean * vn) * phi + (0.5 * skew) * work
+        low = None
+        for k in range(8):
+            a = load(k)
+            node = Node(a[0:3], a[3], a[4], a[6], [0.5 * a[8]] + a[9:13])
+            if k:
+                half_speed = 0.5 * (low.speed + node.speed)
+                for q in range(5):
+                    rate = low.flux[q] + node.flux[q] - half_speed * (node.state[q] - low.state[q])
+                    gained = gained + (0.5 * rate) * (node.cot[q] - low.cot[q])
+            low = node
+        gsum[step] = gained
+        return carry
+
+    lax.fori_loop(0, 6, one, 0)
+
+    half_lane = lax.broadcasted_iota(jnp.int32, (16, 128), 1) >> 6
+    along = jnp.concatenate([gsum[4], gsum[5]], axis=0)
+    factors = msg[...]
+    for h in range(2):
+        row = jnp.sum(gsum[h] + gsum[2 + h], axis=0, keepdims=True)
+        both = jnp.where(half_lane == h, along, 0.0) + jnp.where(spread, row, 0.0)
+        column = jnp.sum(both, axis=1, keepdims=True)
+        gain = jnp.sum(jnp.where(spread, column, 0.0), axis=0, keepdims=True)
+        factors = jnp.where(sub16 == 4 + h, gain, factors)
+        factors = jnp.where(sub16 == 2 + h, gain * (1.0 - factors[h : h + 1]), factors)
+    msg[...] = factors
+    for target, row in ((to_partner, 160), (to_other, 160), (to_ahead, 80), (to_behind, 80)):
+        target[pl.ds(row, 8), :] = factors[0:8]
 
 
 def conserved_node(state, cot, direction):
@@ -435,20 +369,20 @@
     )
 
 
-def near_node(ref, count, start, direction):
-    return conserved_node(
-        [ref[pl.ds(q * count + start, 8), :] for q in range(5)],
-        [ref[pl.ds((5 + q) * count + start, 8), :] for q in range(5)],
-        direction,
-    )
-
-
-def kernel_local(
+def near_node(first, other, choose, count, start, direction):
+    def value(c):
+        rows = pl.ds(c * count + start, 8)
+        return jnp.where(choose, first[rows, :], other[rows, :])
+
+    return conserved_node([value(q) for q in range(5)], [value(5 + q) for q in range(5)], direction)
+
+
+def kernel_second(
     ids_hbm,
     flow,
     cot,
-    parts,
-    zends,
+    lines,
+    mid,
     modes,
     msg,
     tables,
@@ -456,7 +390,9 @@
     extra,
     slope,
     zsum,
+    out,
     zacc,
+    zends,
     znext,
     zback,
     ids,
@@ -465,9 +401,7 @@
     copy = pltpu.make_async_copy(ids_hbm, ids, sem)
     copy.start()
 
-    sub = lax.broadcasted_iota(jnp.int32, (8, 128), 0)
-    lane = lax.broadcasted_iota(jnp.int32, (8, 128), 1)
-    high = (sub >= 6) | ((lane & 7) >= 6)
+    sub, lane, high = lane_tables()
     tiles = []
     for h in range(2):
         d_top = msg[pl.ds(6 + h, 1), :]
@@ -494,6 +428,104 @@
                 slope[1 + i, rows, :] = -(pull_e * vel[i])
             slope[4, rows, :] = pull_e
 
+    def one(step, carry):
+        d = step // 2
+        base = (step % 2) * 64
+
+        def rows(k):
+            return pl.ds(pl.multiple_of(base + 8 * k, 8), 8)
+
+        for k in range(7):
+            a = [lines[d, q, rows(k), :] for q in range(NQ)]
+            acc = [None] * 13 if k == 0 else [out[d, q, rows(k), :] for q in range(13)]
+            for j in range(k + 1, 8):
+                skew = float(SKEW[k, j])
+                half = 0.5 * skew
+                b = [lines[d, q, rows(j), :] for q in range(NQ)]
+                mean, quot, inv5, dot, phi = (mid[step, 5 * PAIR[k, j] + q] for q in range(5))
+                vn, v1, v2, pres = (a[i] + b[i] for i in range(4))
+                delta = [None] + [a[8 + i] - b[8 + i] for i in range(1, 5)]
+                y = a[5] - b[5]
+                slope = (((0.25 * skew) * (a[4] * b[4])) * y) * horner(SLOPE_R, y * y)
+                yb = a[7] - b[7]
+                tilt = yb * (horner(SLOPE_B, yb * yb) * quot)
+                mass = mean * vn
+                flux = [
+                    mass,
+                    mass * vn + half * pres,
+                    mass * v1,
+                    mass * v2,
+                    mass * dot + half * (a[3] * b[0] + b[3] * a[0]),
+                ]
+                t = half * delta[4]
+                w = mass * delta[4]
+                pp = phi * mass
+                qq = (phi * vn) * slope
+                xx = w * inv5
+                zz = xx * tilt
+                shared = [
+                    phi * mean + mass * (delta[1] + delta[4] * vn) + t * pres,
+                    mass * (delta[2] + delta[4] * v1),
+                    mass * (delta[3] + delta[4] * v2),
+                    half * (delta[1] + delta[4] * vn),
+                ]
+                ups = flux + [pp + qq] + shared + [xx + zz, w, t]
+                downs = [None] * 5 + [pp - qq] + shared + [xx - zz, w, t]
+                for q in range(13):
+                    acc[q] = ups[q] if acc[q] is None else acc[q] + ups[q]
+                    if q < 5:
+                        value = -flux[q] if k == 0 else out[d, q, rows(j), :] - flux[q]
+                    else:
+                        value = downs[q] if k == 0 else out[d, q, rows(j), :] + downs[q]
+                    out[d, q, rows(j), :] = value
+            for q in range(13):
+                out[d, q, rows(k), :] = acc[q]
+
+        low = None
+        zero = jnp.zeros((8, 128), F32)
+        low_flux, low_weight, low_direct, low_dot = [zero] * 5, [zero] * 5, [zero] * 5, zero
+        for k in range(9):
+            if k < 8:
+                a = [lines[d, q, rows(k), :] for q in range(NQ)]
+                node = Node(a[0:3], a[3], a[4], a[6], [0.5 * a[8]] + a[9:13])
+            if k == 0:
+                low = node
+                continue
+            if k < 8:
+                flux, weight, direct, dot = face(low, node)
+            else:
+                flux, weight, direct, dot = [zero] * 5, [zero] * 5, [zero] * 5, zero
+            m = k - 1
+            total = [out[d, q, rows(m), :] for q in range(13)]
+            for i in range(3):
+                total[6 + i] = total[6 + i] - total[11] * low.vel[i]
+            total[6] = total[6] - total[12] * low.pres
+            total[9] = total[9] - total[12] * low.vel[0]
+            total[0] = 2.0 * total[0]
+            for q in range(5):
+                diff = total[q] - (flux[q] - low_flux[q])
+                out[d, q, rows(m), :] = total[q] * (-INV_W[m])
+                out[d, 5 + q, rows(m), :] = diff * INV_W[m]
+            fv = low.pull(
+                [0.5 * (x + z) for x, z in zip(low_weight, weight)],
+                [x - z for x, z in zip(direct, low_direct)],
+                low_dot + dot,
+            )
+            inv = rcp(low.state[0])
+            beta = 0.5 * total[10]
+            g_rho = (beta - 0.5 * total[5]) * inv
+            g_e = -0.4 * (total[9] + beta * rcp(low.pres))
+            g_m = [-(total[6 + i] * inv) - g_e * low.vel[i] for i in range(3)]
+            inner = g_m[0] * low.vel[0] + g_m[1] * low.vel[1] + g_m[2] * low.vel[2]
+            dg = [g_rho - inner - (0.5 * g_e) * low.square] + g_m + [g_e]
+            for q in range(5):
+                out[d, 10 + q, rows(m), :] = dg[q]
+                out[d, 15 + q, rows(m), :] = fv[q] - dg[q]
+            low, low_flux, low_weight, low_direct, low_dot = node, flux, weight, direct, dot
+        return carry
+
+    lax.fori_loop(0, 6, one, 0)
+
     copy.wait()
     row = lax.broadcasted_iota(jnp.int32, (128, 128), 0)
     lanes = lax.broadcasted_iota(jnp.int32, (8, 128), 1)
@@ -508,6 +540,10 @@
         own, up, (((1,), (1,)), ((), ())), precision=HIGHEST, preferred_element_type=F32
     )
 
+    for q in range(NQ):
+        for end in range(2):
+            for h in range(2):
+                zends[q, pl.ds(end * 16 + h * 8, 8), :] = lines[2, q, pl.ds(h * 64 + 56 * end, 8), :]
     for k in range(16):
         znext[:, pl.ds(k, 1), :] = zends[:, pl.ds(ids[k], 1), :]
     for h in range(2):
@@ -534,10 +570,9 @@
             pieces = []
             for slot in range(16):
                 h, s = slot // 8, slot % 8
-                pieces.append(parts[2, first + qz, pl.ds(h * 64 + s, 8, stride=8), :])
+                pieces.append(out[2, first + qz, pl.ds(h * 64 + s, 8, stride=8), :])
             if group_at in (0, 2):
                 source = qz + (0 if group_at == 0 else 5)
-                sub = lax.broadcasted_iota(jnp.int32, (8, 128), 0)
                 for slot in range(16):
                     upper = zacc[source, pl.ds(slot, 1), :]
                     lower = zacc[source, pl.ds(16 + slot, 1), :]
@@ -547,8 +582,8 @@
             for h in range(2):
                 for x in range(8):
                     value = (
-                        parts[0, qx, pl.ds(h * 64 + 8 * x, 8), :]
-                        + parts[1, qy, pl.ds(h * 64 + x, 8, stride=8), :]
+                        out[0, qx, pl.ds(h * 64 + 8 * x, 8), :]
+                        + out[1, qy, pl.ds(h * 64 + x, 8, stride=8), :]
                         + whole[h * 64 + 8 * x : h * 64 + 8 * x + 8]
                     )
                     target[offset + q, pl.ds(x * 16 + h * 8, 8), :] = value
@@ -565,10 +600,10 @@
 def kernel_blend(
     msg,
     zsum,
-    from_left,
-    from_right,
-    from_low,
-    from_up,
+    partner,
+    other,
+    ahead,
+    behind,
     flow,
     cot,
     base,
@@ -579,19 +614,18 @@
     total,
     sems,
 ):
+    even_x = lax.axis_index("gx") % 2 == 0
+    even_y = lax.axis_index("gy") % 2 == 0
+    sides = partner[160:168, :] + other[160:168, :]
+    met, left = ahead[80:88, :], behind[80:88, :]
+    above, below = jnp.where(even_y, met, left), jnp.where(even_y, left, met)
     for h in range(2):
 
         def beside_of(i):
             r = 2 * i + h
-            low = from_low[81 + 2 * i : 82 + 2 * i, :] if h == 0 else msg[2 * i : 2 * i + 1, :]
-            high = msg[2 * i + 1 : 2 * i + 2, :] if h == 0 else from_up[80 + 2 * i : 81 + 2 * i, :]
-            return (
-                zsum[r : r + 1, :]
-                + from_left[160 + r : 161 + r, :]
-                + from_right[160 + r : 161 + r, :]
-                + low
-                + high
-            )
+            low = below[2 * i + 1 : 2 * i + 2] if h == 0 else msg[2 * i : 2 * i + 1, :]
+            high = msg[2 * i + 1 : 2 * i + 2, :] if h == 0 else above[2 * i : 2 * i + 1]
+            return zsum[r : r + 1, :] + sides[r : r + 1] + low + high
 
         alpha = msg[h : h + 1, :]
         gain = msg[4 + h : 5 + h, :]
@@ -614,30 +648,50 @@
             total[p, rows, :] += res[q]
             total[5 + p, rows, :] += grad[q]
 
+    here, top = pl.ds(0, 8, stride=16), pl.ds(15, 8, stride=16)
+    shares = face_shares(near_node(behind, ahead, even_y, 8, 0, 1), own_node(flow, cot, 1, here))
+    add(1, here, shares[2], shares[3])
+    shares = face_shares(own_node(flow, cot, 1, top), near_node(ahead, behind, even_y, 8, 0, 1))
+    add(1, top, shares[0], shares[1])
+
+    def send(i, start, count):
+        rows = pl.ds(start, count)
+        return [
+            pltpu.make_async_copy(
+                total.at[pl.ds(0, 5), rows], residual_hbm.at[pl.ds(0, 5), rows], sems.at[2 * i]
+            ),
+            pltpu.make_async_copy(
+                total.at[pl.ds(5, 5), rows], grad_hbm.at[pl.ds(0, 5), rows], sems.at[2 * i + 1]
+            ),
+        ]
+
+    copies = send(0, 16, 96)
+    for copy in copies:
+        copy.start()
     for h in range(2):
         here, top = pl.ds(h * 8, 8), pl.ds(112 + h * 8, 8)
-        shares = face_shares(near_node(from_left, 16, h * 8, 0), own_node(flow, cot, 0, here))
+        shares = face_shares(
+            near_node(other, partner, even_x, 16, h * 8, 0), own_node(flow, cot, 0, here)
+        )
         add(0, here, shares[2], shares[3])
-        shares = face_shares(own_node(flow, cot, 0, top), near_node(from_right, 16, h * 8, 0))
+        shares = face_shares(
+            own_node(flow, cot, 0, top), near_node(partner, other, even_x, 16, h * 8, 0)
+        )
         add(0, top, shares[0], shares[1])
-    here, top = pl.ds(0, 8, stride=16), pl.ds(15, 8, stride=16)
-    shares = face_shares(near_node(from_low, 8, 0, 1), own_node(flow, cot, 1, here))
-    add(1, here, shares[2], shares[3])
-    shares = face_shares(own_node(flow, cot, 1, top), near_node(from_up, 8, 0, 1))
-    add(1, top, shares[0], shares[1])
-    copies = [
-        pltpu.make_async_copy(total.at[pl.ds(0, 5)], residual_hbm, sems.at[0]),
-        pltpu.make_async_copy(total.at[pl.ds(5, 5)], grad_hbm, sems.at[1]),
-    ]
-    for copy in copies:
+    last = send(1, 0, 16) + send(2, 112, 16)
+    for copy in last:
         copy.start()
-    for copy in copies:
+    for copy in copies + last:
         copy.wait()
 
 
-def shifted(value, axis, steps):
+def swapped(value, axis, first):
     count = lax.axis_size(axis)
-    return lax.ppermute(value, axis, [(i, (i + steps) % count) for i in range(count)])
+    pairs = []
+    for i in range(first, count + first, 2):
+        a, b = i % count, (i + 1) % count
+        pairs += [(a, b), (b, a)]
+    return lax.ppermute(value, axis, pairs)
 
 
 def shape(*dims):
@@ -658,11 +712,11 @@
     kz = np.kron(np.eye(16), modal).astype(np.float32)
     constants = np.stack([kxy, kz.T, kxy.T, kz])
 
-    parts, zends, modes, msg, to_right, to_left, to_up, to_low, flow_v, cot_v, tables = pl.pallas_call(
-        kernel_volume,
+    lines, mid, modes, msg, to_partner, to_other, to_ahead, to_behind, flow_v, cot_v, tables = pl.pallas_call(
+        kernel_first,
         out_shape=(
-            shape(3, 20, ROWS, 128),
-            shape(NQ, 32, 128),
+            shape(3, NQ, ROWS, 128),
+            shape(6, 5 * 28, 8, 128),
             shape(ROWS, 128),
             shape(16, 128),
             shape(168, 128),
@@ -678,46 +732,47 @@
         scratch_shapes=[
             pltpu.VMEM((NQ, ROWS, 128), F32),
             pltpu.VMEM((NQ, ROWS, 128), F32),
-            pltpu.VMEM((3, NQ, ROWS, 128), F32),
             pltpu.VMEM((ROWS, 128), F32),
             pltpu.VMEM((6, 8, 128), F32),
             pltpu.VMEM((2, 16), jnp.int32),
             pltpu.SemaphoreType.DMA((4,)),
         ],
-        compiler_params=pltpu.CompilerParams(vmem_limit_bytes=20 * 1024 * 1024),
-        name="volume",
+        compiler_params=pltpu.CompilerParams(vmem_limit_bytes=16 * 1024 * 1024),
+        name="first",
     )(in_hbm(flow), in_hbm(cot), in_hbm(clip_flags.reshape(2, 16)), in_hbm(jnp.asarray(constants)))
 
-    from_low = shifted(to_up, "gy", 1)
-    from_up = shifted(to_low, "gy", -1)
-    from_left = shifted(to_right, "gx", 1)
-    from_right = shifted(to_left, "gx", -1)
+    ahead = swapped(to_ahead, "gy", 0)
+    behind = swapped(to_behind, "gy", 1)
+    other = swapped(to_other, "gx", 1)
+    partner = swapped(to_partner, "gx", 0)
 
     base, extra, slope, zsum = pl.pallas_call(
-        kernel_local,
+        kernel_second,
         out_shape=(shape(10, ROWS, 128), shape(10, ROWS, 128), shape(5, ROWS, 128), shape(8, 128)),
         in_specs=[hbm] + [vmem] * 7,
         out_specs=[vmem] * 4,
         scratch_shapes=[
+            pltpu.VMEM((3, 20, ROWS, 128), F32),
             pltpu.VMEM((10, 32, 128), F32),
+            pltpu.VMEM((NQ, 32, 128), F32),
             pltpu.VMEM((NQ, 16, 128), F32),
             pltpu.VMEM((10, 16, 128), F32),
             pltpu.SMEM((16,), jnp.int32),
             pltpu.SemaphoreType.DMA(()),
         ],
         compiler_params=pltpu.CompilerParams(vmem_limit_bytes=16 * 1024 * 1024),
-        name="local",
-    )(in_hbm(successor_ids), flow_v, cot_v, parts, zends, modes, msg, tables)
+        name="second",
+    )(in_hbm(successor_ids), flow_v, cot_v, lines, mid, modes, msg, tables)
 
     residual, grad = pl.pallas_call(
         kernel_blend,
         out_shape=(shape(5, ROWS, 128), shape(5, ROWS, 128)),
         in_specs=[vmem] * 11,
         out_specs=[hbm] * 2,
-        scratch_shapes=[pltpu.VMEM((10, ROWS, 128), F32), pltpu.SemaphoreType.DMA((2,))],
+        scratch_shapes=[pltpu.VMEM((10, ROWS, 128), F32), pltpu.SemaphoreType.DMA((6,))],
         compiler_params=pltpu.CompilerParams(vmem_limit_bytes=16 * 1024 * 1024),
         name="blend",
-    )(msg, zsum, from_left, from_right, from_low, from_up, flow_v, cot_v, base, extra, slope)
+    )(msg, zsum, partner, other, ahead, behind, flow_v, cot_v, base, extra, slope)
     return residual.reshape(flow_state.shape), grad.reshape(flow_state.shape)
 
 

time: 26.1 us -> 23.8 us (0.912)
  the two profiles are of different devices: /device:TPU:64 before, /device:TPU:32 now
where the time goes in v2:
time: 23.8 us; the launch traced here: 23.7 us
  starting transfers between devices  12.7 us (53%)
  Pallas kernels  10.3 us (43%)
  between operations  0.69 us (3%)
    ppermute x4, starting transfers between devices, swapped(): return lax.ppermute(value, axis, pairs)  12.7 us
    pallas_call x1, Pallas kernels, shards(): pl.pallas_call(kernel_second, out_shape=(shape(10, ROWS, 128), shape(10,...  4.95 us
    pallas_call x1, Pallas kernels, shards(): pl.pallas_call(kernel_first, out_shape=(shape(3, NQ, ROWS, 128), shape(6,...  4.2 us
    pallas_call x1, Pallas kernels, shards(): pl.pallas_call(kernel_blend, out_shape=(shape(5, ROWS, 128), shape(5, ROW...  1.14 us
  transfers between devices with their start and end apart: 4, of which 0 were waited for; matrix products, arithmetic and copies ran while one was open for 0% of the time, Pallas kernels for 21%

profile of v2, /device:TPU:32, one launch (start us, length us, event | category | flops | bytes accessed | tf_op | source)
XLA Modules:
  0.0 23.7 jit_solution(5806167182901243269)
XLA Ops:
  0.6 4.2 %first.1 = (f32[3,13,128,128]{3,2,1,0:T(8,128)S(1)}, f32[6,140,8,128]{3,2,1,0:T(8,128)S(1)}, f32[128,128]{1,0:T(8,128)S(1)}, f32[16,128]{1,0:T(8,128)S(1)}, f32[...) custom-call(f32[5,128,128]{2,1,0:T(8,128)} %bitcast.5, ...), custom_call_target="tpu_custom_call" | custom-call | tf_op jit(solution)/shard_map/first/pallas_call | solution.py:715
  4.8 0.1 collective-permute-start
  4.9 4.9 %collective-permute-start.1 = (f32[168,128]{1,0:T(8,128)S(1)}, f32[168,128]{1,0:T(8,128)S(1)}, u32[]{:S(2)}, u32[]{:S(2)}) collective-permute-start(f32[168,128]{1,0:T(8,128)S(1)} %get-tuple-element.28), channel_id=1, source_target_pairs={{4,8},{8,4},{12,16},{16,12},{20,24},{24,20},{28,32},{32,28},{36,40... | collective-permute-start | bytes 258056 | tf_op jit(solution)/shard_map/ppermute | solution.py:694
  9.8 3.3 %collective-permute-start.2 = (f32[88,128]{1,0:T(8,128)S(1)}, f32[88,128]{1,0:T(8,128)S(1)}, u32[]{:S(2)}, u32[]{:S(2)}) collective-permute-start(f32[88,128]{1,0:T(8,128)S(1)} %get-tuple-element.29), channel_id=1, source_target_pairs={{0,1},{1,0},{2,3},{3,2},{4,5},{5,4},{6,7},{7,6},{8,9},{9,8},{10,11... | collective-permute-start | bytes 135176 | tf_op jit(solution)/shard_map/ppermute | solution.py:694
  13.1 4.5 %collective-permute-start.3 = (f32[88,128]{1,0:T(8,128)S(1)}, f32[88,128]{1,0:T(8,128)S(1)}, u32[]{:S(2)}, u32[]{:S(2)}) collective-permute-start(f32[88,128]{1,0:T(8,128)S(1)} %get-tuple-element.30), channel_id=1, source_target_pairs={{1,2},{2,1},{3,0},{0,3},{5,6},{6,5},{7,4},{4,7},{9,10},{10,9},{11,... | collective-permute-start | bytes 135176 | tf_op jit(solution)/shard_map/ppermute | solution.py:694
  17.6 5.0 %second.1 = (f32[10,128,128]{2,1,0:T(8,128)S(1)}, f32[10,128,128]{2,1,0:T(8,128)S(1)}, f32[5,128,128]{2,1,0:T(8,128)S(1)}, f32[8,128]{1,0:T(8,128)S(1)}) custom-call(s32[16]{0:T(128)} %ids_hbm.1, f32[5,128,128]{2,1,0:T(8,128)S(1)} %get-tuple-element.20.flow, f32[5,128,128]{2,1,0:T(8,128)S(1)} %get-tuple-element.21.cot, ...), custom_call_target="tpu_custom_call" | custom-call | tf_op jit(solution)/shard_map/second/pallas_call | solution.py:749
  22.5 0.0 collective-permute-done.2.ahead
  22.5 0.0 collective-permute-done.3.behind
  22.5 0.0 collective-permute-done.partner
  22.5 0.0 collective-permute-done.1.other
  22.6 1.1 %blend.1 = (f32[5,128,128]{2,1,0:T(8,128)}, f32[5,128,128]{2,1,0:T(8,128)}) custom-call(f32[16,128]{1,0:T(8,128)S(1)} %get-tuple-element.19.msg, f32[8,128]{1,0:T(8,128)S(1)} %get-tuple-element.26.zsum, f32[168,128]{1,0:T(8,128)S(1)} %collective-permute-done.partner, f32[168,128]{1,0:T(8,128)S(1)} %collective-permute-done.1.other, ...), custom_call_target="tpu_custom_call" | custom-call | tf_op jit(solution)/shard_map/blend/pallas_call | solution.py:767
Async XLA Ops:
  4.8 17.7 %collective-permute-start = (f32[168,128]{1,0:T(8,128)S(1)}, f32[168,128]{1,0:T(8,128)S(1)}, u32[]{:S(2)}, u32[]{:S(2)}) collective-permute-start(f32[168,128]{1,0:T(8,128)S(1)} %get-tuple-element.27), channel_id=1, source_target_pairs={{0,4},{4,0},{8,12},{12,8},{16,20},{20,16},{24,28},{28,24},{32,36},... | collective-permute-start | bytes 258056 | tf_op jit(solution)/shard_map/ppermute | solution.py:694
  4.9 17.6 %collective-permute-start.1 = (f32[168,128]{1,0:T(8,128)S(1)}, f32[168,128]{1,0:T(8,128)S(1)}, u32[]{:S(2)}, u32[]{:S(2)}) collective-permute-start(f32[168,128]{1,0:T(8,128)S(1)} %get-tuple-element.28), channel_id=1, source_target_pairs={{4,8},{8,4},{12,16},{16,12},{20,24},{24,20},{28,32},{32,28},{36,40... | collective-permute-start | bytes 258056 | tf_op jit(solution)/shard_map/ppermute | solution.py:694
  9.8 12.7 %collective-permute-start.2 = (f32[88,128]{1,0:T(8,128)S(1)}, f32[88,128]{1,0:T(8,128)S(1)}, u32[]{:S(2)}, u32[]{:S(2)}) collective-permute-start(f32[88,128]{1,0:T(8,128)S(1)} %get-tuple-element.29), channel_id=1, source_target_pairs={{0,1},{1,0},{2,3},{3,2},{4,5},{5,4},{6,7},{7,6},{8,9},{9,8},{10,11... | collective-permute-start | bytes 135176 | tf_op jit(solution)/shard_map/ppermute | solution.py:694
  13.1 9.5 %collective-permute-start.3 = (f32[88,128]{1,0:T(8,128)S(1)}, f32[88,128]{1,0:T(8,128)S(1)}, u32[]{:S(2)}, u32[]{:S(2)}) collective-permute-start(f32[88,128]{1,0:T(8,128)S(1)} %get-tuple-element.30), channel_id=1, source_target_pairs={{1,2},{2,1},{3,0},{0,3},{5,6},{6,5},{7,4},{4,7},{9,10},{10,9},{11,... | collective-permute-start | bytes 135176 | tf_op jit(solution)/shard_map/ppermute | solution.py:694

commit v3 on v2

--- a/solution.py
+++ b/solution.py
@@ -73,6 +73,7 @@
     return np.where(square < 1e-2, series, exact)
 
 
+RATES = 5 * 28
 PAIR = {pair: i for i, pair in enumerate((k, j) for k in range(7) for j in range(k + 1, 8))}
 
 MEAN_R = fitted(sinhc, 3.0, 4)
@@ -140,16 +141,21 @@
         return grad
 
 
-def face(low, up):
+def face_adjoint(low, up):
     jump = [b - a for a, b in zip(low.state, up.state)]
     weight = [b - a for a, b in zip(low.cot, up.cot)]
-    half_speed = 0.25 * (low.speed + up.speed)
-    flux = [0.5 * (a + b) - half_speed * j for a, b, j in zip(low.flux, up.flux, jump)]
+    speed = 0.5 * (low.speed + up.speed)
     dot = weight[0] * jump[0]
     for i in range(1, 5):
         dot = dot + weight[i] * jump[i]
-    direct = [half_speed * w for w in weight]
-    return flux, weight, direct, -0.25 * dot
+    return weight, [speed * w for w in weight], -0.5 * dot
+
+
+def face_rate(low, up):
+    speed = 0.5 * (low.speed + up.speed)
+    return [
+        a + b - speed * (y - x) for a, b, x, y in zip(low.flux, up.flux, low.state, up.state)
+    ]
 
 
 def lane_tables():
@@ -174,6 +180,7 @@
     flow,
     cot,
     tables,
+    out,
     nat,
     turned,
     prod,
@@ -191,8 +198,8 @@
         copy.start()
     even_x = lax.axis_index("gx") % 2 == 0
     even_y = lax.axis_index("gy") % 2 == 0
-    copies[0].wait()
-    copies[1].wait()
+    for copy in copies:
+        copy.wait()
     for c in range(10):
         source, q = (flow, c) if c < 5 else (cot, c - 5)
         top, low = source[q, pl.ds(112, 16), :], source[q, pl.ds(0, 16), :]
@@ -230,10 +237,8 @@
                 for k in range(8):
                     rows = pl.ds(h * 64 + 8 * k, 8) if d == 0 else pl.ds(h * 64 + k, 8, stride=8)
                     value = source[order[q], rows, :]
-                    lines[d, q, pl.ds(h * 64 + 8 * k, 8), :] = value * INV_W[k] if q >= 8 else value
-
-    copies[2].wait()
-    copies[3].wait()
+                    lines[d, q, pl.ds(h * 64 + 8 * k, 8), :] = value * (0.5 * INV_W[k]) if q >= 8 else value
+
     sub, lane, high = lane_tables()
     coeffs = jnp.dot(tables[0], prod[...], precision=HIGHEST, preferred_element_type=F32)
     coeffs = jnp.dot(coeffs, tables[1], precision=HIGHEST, preferred_element_type=F32)
@@ -297,7 +302,7 @@
                 vn, v1, v2 = (a[i] + b[i] for i in range(3))
                 delta = [a[8 + i] - b[8 + i] for i in range(5)]
                 y = a[5] - b[5]
-                mean = ((0.25 * skew) * (a[4] * b[4])) * horner(MEAN_R, y * y)
+                mean = ((0.5 * skew) * (a[4] * b[4])) * horner(MEAN_R, y * y)
                 yb = a[7] - b[7]
                 quot = rcp(horner(MEAN_B, yb * yb))
                 inv5 = (a[6] * b[6]) * quot
@@ -306,16 +311,15 @@
                 for q, value in enumerate((mean, quot, inv5, dot, phi)):
                     mid[step, 5 * PAIR[k, j] + q] = value
                 work = delta[1] * (a[3] + b[3]) + delta[4] * (a[3] * b[0] + b[3] * a[0])
-                gained = gained + (mean * vn) * phi + (0.5 * skew) * work
+                gained = gained + (mean * vn) * phi + skew * work
         low = None
         for k in range(8):
             a = load(k)
             node = Node(a[0:3], a[3], a[4], a[6], [0.5 * a[8]] + a[9:13])
             if k:
-                half_speed = 0.5 * (low.speed + node.speed)
-                for q in range(5):
-                    rate = low.flux[q] + node.flux[q] - half_speed * (node.state[q] - low.state[q])
-                    gained = gained + (0.5 * rate) * (node.cot[q] - low.cot[q])
+                for q, rate in enumerate(face_rate(low, node)):
+                    mid[step, RATES + 5 * (k - 1) + q] = rate
+                    gained = gained + rate * (node.cot[q] - low.cot[q])
             low = node
         gsum[step] = gained
         return carry
@@ -336,6 +340,12 @@
     for target, row in ((to_partner, 160), (to_other, 160), (to_ahead, 80), (to_behind, 80)):
         target[pl.ds(row, 8), :] = factors[0:8]
 
+    def two(step, carry):
+        adjoint_step(lines, mid, out, step)
+        return carry
+
+    lax.fori_loop(0, steps_ahead(), two, 0)
+
 
 def conserved_node(state, cot, direction):
     perm = PERMS[direction]
@@ -345,18 +355,121 @@
     square = vel[0] * vel[0] + vel[1] * vel[1] + vel[2] * vel[2]
     pres = 0.4 * (state[4] - 0.5 * density * square)
     scaled = [cot[0]] + [cot[1 + i] for i in perm] + [cot[4]]
-    return Node(vel, pres, jnp.sqrt(density), jnp.sqrt(5.0 * pres * inv), [c * INV_W[0] for c in scaled])
+    return Node(vel, pres, jnp.sqrt(density), jnp.sqrt(5.0 * pres * inv), [c * (0.5 * INV_W[0]) for c in scaled])
 
 
 def face_shares(low, up):
-    flux, weight, direct, dot = face(low, up)
-    half = [0.5 * w for w in weight]
+    rate = face_rate(low, up)
+    weight, direct, dot = face_adjoint(low, up)
     return (
-        [-INV_W[7] * f for f in flux],
-        low.pull(half, direct, dot),
-        [INV_W[0] * f for f in flux],
-        up.pull(half, [-x for x in direct], dot),
+        [(-0.5 * INV_W[7]) * f for f in rate],
+        low.pull(weight, direct, dot),
+        [(0.5 * INV_W[0]) * f for f in rate],
+        up.pull(weight, [-x for x in direct], dot),
     )
+
+
+def steps_ahead():
+    gx = lax.axis_index("gx")
+    plane = 2 * lax.axis_index("gy") + gx // 32
+    corner = jnp.where(plane < 4, jnp.minimum(6 - plane, 5), 0)
+    return jnp.where(gx % 32 == 0, corner, jnp.where(plane < 2, 5 - plane, 0))
+
+
+def adjoint_step(lines, mid, out, step):
+    d = step // 2
+    base = (step % 2) * 64
+
+    def rows(k):
+        return pl.ds(pl.multiple_of(base + 8 * k, 8), 8)
+
+    for k in range(7):
+        a = [lines[d, q, rows(k), :] for q in range(NQ)]
+        acc = [None] * 13 if k == 0 else [out[d, q, rows(k), :] for q in range(13)]
+        for j in range(k + 1, 8):
+            skew = float(SKEW[k, j])
+            b = [lines[d, q, rows(j), :] for q in range(NQ)]
+            mean, quot, inv5, dot, phi = (mid[step, 5 * PAIR[k, j] + q] for q in range(5))
+            vn, v1, v2, pres = (a[i] + b[i] for i in range(4))
+            delta = [None] + [a[8 + i] - b[8 + i] for i in range(1, 5)]
+            y = a[5] - b[5]
+            slope = (((0.5 * skew) * (a[4] * b[4])) * y) * horner(SLOPE_R, y * y)
+            yb = a[7] - b[7]
+            tilt = yb * (horner(SLOPE_B, yb * yb) * quot)
+            mass = mean * vn
+            flux = [
+                mass,
+                mass * vn + skew * pres,
+                mass * v1,
+                mass * v2,
+                mass * dot + skew * (a[3] * b[0] + b[3] * a[0]),
+            ]
+            t = skew * delta[4]
+            w = mass * delta[4]
+            pp = phi * mass
+            qq = (phi * vn) * slope
+            xx = w * inv5
+            zz = xx * tilt
+            shared = [
+                phi * mean + mass * (delta[1] + delta[4] * vn) + t * pres,
+                mass * (delta[2] + delta[4] * v1),
+                mass * (delta[3] + delta[4] * v2),
+                skew * (delta[1] + delta[4] * vn),
+            ]
+            ups = flux + [pp + qq] + shared + [xx + zz, w, t]
+            downs = [None] * 5 + [pp - qq] + shared + [xx - zz, w, t]
+            for q in range(13):
+                acc[q] = ups[q] if acc[q] is None else acc[q] + ups[q]
+                if q < 5:
+                    value = -flux[q] if k == 0 else out[d, q, rows(j), :] - flux[q]
+                else:
+                    value = downs[q] if k == 0 else out[d, q, rows(j), :] + downs[q]
+                out[d, q, rows(j), :] = value
+        for q in range(13):
+            out[d, q, rows(k), :] = acc[q]
+
+    low = None
+    zero = jnp.zeros((8, 128), F32)
+    low_flux, low_weight, low_direct, low_dot = [zero] * 5, [zero] * 5, [zero] * 5, zero
+    for k in range(9):
+        if k < 8:
+            a = [lines[d, q, rows(k), :] for q in range(NQ)]
+            node = Node(a[0:3], a[3], a[4], a[6], [0.5 * a[8]] + a[9:13])
+        if k == 0:
+            low = node
+            continue
+        if k < 8:
+            weight, direct, dot = face_adjoint(low, node)
+            flux = [mid[step, RATES + 5 * (k - 1) + q] for q in range(5)]
+        else:
+            flux, weight, direct, dot = [zero] * 5, [zero] * 5, [zero] * 5, zero
+        m = k - 1
+        total = [out[d, q, rows(m), :] for q in range(13)]
+        for i in range(3):
+            total[6 + i] = total[6 + i] - total[11] * low.vel[i]
+        total[6] = total[6] - total[12] * low.pres
+        total[9] = total[9] - total[12] * low.vel[0]
+        total[0] = 2.0 * total[0]
+        for q in range(5):
+            diff = total[q] - (flux[q] - low_flux[q])
+            out[d, q, rows(m), :] = total[q] * (-0.5 * INV_W[m])
+            out[d, 5 + q, rows(m), :] = diff * (0.5 * INV_W[m])
+        fv = low.pull(
+            [x + z for x, z in zip(low_weight, weight)],
+            [x - z for x, z in zip(direct, low_direct)],
+            low_dot + dot,
+        )
+        inv = rcp(low.state[0])
+        beta = 0.5 * total[10]
+        g_rho = (beta - 0.5 * total[5]) * inv
+        g_e = -0.4 * (total[9] + beta * rcp(low.pres))
+        g_m = [-(total[6 + i] * inv) - g_e * low.vel[i] for i in range(3)]
+        inner = g_m[0] * low.vel[0] + g_m[1] * low.vel[1] + g_m[2] * low.vel[2]
+        dg = [g_rho - inner - (0.5 * g_e) * low.square] + g_m + [g_e]
+        for q in range(5):
+            out[d, 10 + q, rows(m), :] = dg[q]
+            out[d, 15 + q, rows(m), :] = fv[q] - dg[q]
+        low, low_flux, low_weight, low_direct, low_dot = node, flux, weight, direct, dot
 
 
 def place(d, q):
@@ -386,6 +499,7 @@
     modes,
     msg,
     tables,
+    ahead_sums,
     base,
     extra,
     slope,
@@ -401,6 +515,11 @@
     copy = pltpu.make_async_copy(ids_hbm, ids, sem)
     copy.start()
 
+    def one(step, carry):
+        adjoint_step(lines, mid, out, step)
+        return carry
+
+    lax.fori_loop(steps_ahead(), 6, one, 0)
     sub, lane, high = lane_tables()
     tiles = []
     for h in range(2):
@@ -428,140 +547,8 @@
                 slope[1 + i, rows, :] = -(pull_e * vel[i])
             slope[4, rows, :] = pull_e
 
-    def one(step, carry):
-        d = step // 2
-        base = (step % 2) * 64
-
-        def rows(k):
-            return pl.ds(pl.multiple_of(base + 8 * k, 8), 8)
-
-        for k in range(7):
-            a = [lines[d, q, rows(k), :] for q in range(NQ)]
-            acc = [None] * 13 if k == 0 else [out[d, q, rows(k), :] for q in range(13)]
-            for j in range(k + 1, 8):
-                skew = float(SKEW[k, j])
-                half = 0.5 * skew
-                b = [lines[d, q, rows(j), :] for q in range(NQ)]
-                mean, quot, inv5, dot, phi = (mid[step, 5 * PAIR[k, j] + q] for q in range(5))
-                vn, v1, v2, pres = (a[i] + b[i] for i in range(4))
-                delta = [None] + [a[8 + i] - b[8 + i] for i in range(1, 5)]
-                y = a[5] - b[5]
-                slope = (((0.25 * skew) * (a[4] * b[4])) * y) * horner(SLOPE_R, y * y)
-                yb = a[7] - b[7]
-                tilt = yb * (horner(SLOPE_B, yb * yb) * quot)
-                mass = mean * vn
-                flux = [
-                    mass,
-                    mass * vn + half * pres,
-                    mass * v1,
-                    mass * v2,
-                    mass * dot + half * (a[3] * b[0] + b[3] * a[0]),
-                ]
-                t = half * delta[4]
-                w = mass * delta[4]
-                pp = phi * mass
-                qq = (phi * vn) * slope
-                xx = w * inv5
-                zz = xx * tilt
-                shared = [
-                    phi * mean + mass * (delta[1] + delta[4] * vn) + t * pres,
-                    mass * (delta[2] + delta[4] * v1),
-                    mass * (delta[3] + delta[4] * v2),
-                    half * (delta[1] + delta[4] * vn),
-                ]
-                ups = flux + [pp + qq] + shared + [xx + zz, w, t]
-                downs = [None] * 5 + [pp - qq] + shared + [xx - zz, w, t]
-                for q in range(13):
-                    acc[q] = ups[q] if acc[q] is None else acc[q] + ups[q]
-                    if q < 5:
-                        value = -flux[q] if k == 0 else out[d, q, rows(j), :] - flux[q]
-                    else:
-                        value = downs[q] if k == 0 else out[d, q, rows(j), :] + downs[q]
-                    out[d, q, rows(j), :] = value
-            for q in range(13):
-                out[d, q, rows(k), :] = acc[q]
-
-        low = None
-        zero = jnp.zeros((8, 128), F32)
-        low_flux, low_weight, low_direct, low_dot = [zero] * 5, [zero] * 5, [zero] * 5, zero
-        for k in range(9):
-            if k < 8:
-                a = [lines[d, q, rows(k), :] for q in range(NQ)]
-                node = Node(a[0:3], a[3], a[4], a[6], [0.5 * a[8]] + a[9:13])
-            if k == 0:
-                low = node
-                continue
-            if k < 8:
-                flux, weight, direct, dot = face(low, node)
-            else:
-                flux, weight, direct, dot = [zero] * 5, [zero] * 5, [zero] * 5, zero
-            m = k - 1
-            total = [out[d, q, rows(m), :] for q in range(13)]
-            for i in range(3):
-                total[6 + i] = total[6 + i] - total[11] * low.vel[i]
-            total[6] = total[6] - total[12] * low.pres
-            total[9] = total[9] - total[12] * low.vel[0]
-            total[0] = 2.0 * total[0]
-            for q in range(5):
-                diff = total[q] - (flux[q] - low_flux[q])
-                out[d, q, rows(m), :] = total[q] * (-INV_W[m])
-                out[d, 5 + q, rows(m), :] = diff * INV_W[m]
-            fv = low.pull(
-                [0.5 * (x + z) for x, z in zip(low_weight, weight)],
-                [x - z for x, z in zip(direct, low_direct)],
-                low_dot + dot,
-            )
-            inv = rcp(low.state[0])
-            beta = 0.5 * total[10]
-            g_rho = (beta - 0.5 * total[5]) * inv
-            g_e = -0.4 * (total[9] + beta * rcp(low.pres))
-            g_m = [-(total[6 + i] * inv) - g_e * low.vel[i] for i in range(3)]
-            inner = g_m[0] * low.vel[0] + g_m[1] * low.vel[1] + g_m[2] * low.vel[2]
-            dg = [g_rho - inner - (0.5 * g_e) * low.square] + g_m + [g_e]
-            for q in range(5):
-                out[d, 10 + q, rows(m), :] = dg[q]
-                out[d, 15 + q, rows(m), :] = fv[q] - dg[q]
-            low, low_flux, low_weight, low_direct, low_dot = node, flux, weight, direct, dot
-        return carry
-
-    lax.fori_loop(0, 6, one, 0)
-
-    copy.wait()
-    row = lax.broadcasted_iota(jnp.int32, (128, 128), 0)
-    lanes = lax.broadcasted_iota(jnp.int32, (8, 128), 1)
-    above = jnp.zeros((8, 128), jnp.int32)
-    for k in range(16):
-        above = jnp.where((lanes >> 3) == k, ids[k], above)
-    above = above * 8 + (lanes & 7)
-    above = jnp.concatenate([above] * 16, axis=0)
-    up = jnp.where(above == row, 1.0, 0.0)
-    own = msg[0:8, :]
-    zsum[...] = jnp.dot(own, up, precision=HIGHEST, preferred_element_type=F32) + lax.dot_general(
-        own, up, (((1,), (1,)), ((), ())), precision=HIGHEST, preferred_element_type=F32
-    )
-
-    for q in range(NQ):
-        for end in range(2):
-            for h in range(2):
-                zends[q, pl.ds(end * 16 + h * 8, 8), :] = lines[2, q, pl.ds(h * 64 + 56 * end, 8), :]
-    for k in range(16):
-        znext[:, pl.ds(k, 1), :] = zends[:, pl.ds(ids[k], 1), :]
-    for h in range(2):
-        def side(ref, start):
-            v = [ref[q, pl.ds(start + h * 8, 8), :] for q in range(NQ)]
-            return Node(v[0:3], v[3], v[4], v[6], [0.5 * v[8]] + v[9:13])
-
-        low_r, low_g, up_r, up_g = face_shares(side(zends, 16), side(znext, 0))
-        for q in range(5):
-            zacc[q, pl.ds(h * 8, 8), :] = low_r[q]
-            zacc[5 + q, pl.ds(h * 8, 8), :] = low_g[q]
-            zback[q, pl.ds(h * 8, 8), :] = up_r[q]
-            zback[5 + q, pl.ds(h * 8, 8), :] = up_g[q]
-    for k in range(16):
-        zacc[:, pl.ds(16 + ids[k], 1), :] = zback[:, pl.ds(k, 1), :]
-
     back = [[place(d, q) for q in range(5)] for d in range(3)]
-    for group_at, target, offset in ((0, base, 0), (1, extra, 0), (2, base, 5), (3, extra, 5)):
+    def combine(group_at, target, offset):
         for q in range(5):
             first = group_at * 5
             qx = first + back[0].index(q)
@@ -588,6 +575,46 @@
                     )
                     target[offset + q, pl.ds(x * 16 + h * 8, 8), :] = value
 
+    combine(1, extra, 0)
+    combine(3, extra, 5)
+
+    copy.wait()
+    row = lax.broadcasted_iota(jnp.int32, (128, 128), 0)
+    lanes = lax.broadcasted_iota(jnp.int32, (8, 128), 1)
+    above = jnp.zeros((8, 128), jnp.int32)
+    for k in range(16):
+        above = jnp.where((lanes >> 3) == k, ids[k], above)
+    above = above * 8 + (lanes & 7)
+    above = jnp.concatenate([above] * 16, axis=0)
+    up = jnp.where(above == row, 1.0, 0.0)
+    own = msg[0:8, :]
+    zsum[...] = jnp.dot(own, up, precision=HIGHEST, preferred_element_type=F32) + lax.dot_general(
+        own, up, (((1,), (1,)), ((), ())), precision=HIGHEST, preferred_element_type=F32
+    )
+
+    for q in range(NQ):
+        for end in range(2):
+            for h in range(2):
+                zends[q, pl.ds(end * 16 + h * 8, 8), :] = lines[2, q, pl.ds(h * 64 + 56 * end, 8), :]
+    for k in range(16):
+        znext[:, pl.ds(k, 1), :] = zends[:, pl.ds(ids[k], 1), :]
+    for h in range(2):
+        def side(ref, start):
+            v = [ref[q, pl.ds(start + h * 8, 8), :] for q in range(NQ)]
+            return Node(v[0:3], v[3], v[4], v[6], [0.5 * v[8]] + v[9:13])
+
+        low_r, low_g, up_r, up_g = face_shares(side(zends, 16), side(znext, 0))
+        for q in range(5):
+            zacc[q, pl.ds(h * 8, 8), :] = low_r[q]
+            zacc[5 + q, pl.ds(h * 8, 8), :] = low_g[q]
+            zback[q, pl.ds(h * 8, 8), :] = up_r[q]
+            zback[5 + q, pl.ds(h * 8, 8), :] = up_g[q]
+    for k in range(16):
+        zacc[:, pl.ds(16 + ids[k], 1), :] = zback[:, pl.ds(k, 1), :]
+
+    combine(0, base, 0)
+    combine(2, base, 5)
+
     rows = [pl.ds(7, 8, stride=16), pl.ds(8, 8, stride=16)]
     shares = face_shares(own_node(flow, cot, 1, rows[0]), own_node(flow, cot, 1, rows[1]))
     for side in range(2):
@@ -712,11 +739,11 @@
     kz = np.kron(np.eye(16), modal).astype(np.float32)
     constants = np.stack([kxy, kz.T, kxy.T, kz])
 
-    lines, mid, modes, msg, to_partner, to_other, to_ahead, to_behind, flow_v, cot_v, tables = pl.pallas_call(
+    lines, mid, modes, msg, to_partner, to_other, to_ahead, to_behind, flow_v, cot_v, tables, sums = pl.pallas_call(
         kernel_first,
         out_shape=(
             shape(3, NQ, ROWS, 128),
-            shape(6, 5 * 28, 8, 128),
+            shape(6, RATES + 35, 8, 128),
             shape(ROWS, 128),
             shape(16, 128),
             shape(168, 128),
@@ -726,9 +753,10 @@
             shape(5, ROWS, 128),
             shape(5, ROWS, 128),
             shape(4, 128, 128),
+            shape(3, 20, ROWS, 128),
         ),
         in_specs=[hbm] * 4,
-        out_specs=[vmem] * 11,
+        out_specs=[vmem] * 12,
         scratch_shapes=[
             pltpu.VMEM((NQ, ROWS, 128), F32),
             pltpu.VMEM((NQ, ROWS, 128), F32),
@@ -746,13 +774,13 @@
     other = swapped(to_other, "gx", 1)
     partner = swapped(to_partner, "gx", 0)
 
-    base, extra, slope, zsum = pl.pallas_call(
+    base, extra, slope, zsum, _ = pl.pallas_call(
         kernel_second,
-        out_shape=(shape(10, ROWS, 128), shape(10, ROWS, 128), shape(5, ROWS, 128), shape(8, 128)),
-        in_specs=[hbm] + [vmem] * 7,
-        out_specs=[vmem] * 4,
+        out_shape=(shape(10, ROWS, 128), shape(10, ROWS, 128), shape(5, ROWS, 128), shape(8, 128), shape(3, 20, ROWS, 128)),
+        in_specs=[hbm] + [vmem] * 8,
+        out_specs=[vmem] * 5,
+        input_output_aliases={8: 4},
         scratch_shapes=[
-            pltpu.VMEM((3, 20, ROWS, 128), F32),
             pltpu.VMEM((10, 32, 128), F32),
             pltpu.VMEM((NQ, 32, 128), F32),
             pltpu.VMEM((NQ, 16, 128), F32),
@@ -762,7 +790,7 @@
         ],
         compiler_params=pltpu.CompilerParams(vmem_limit_bytes=16 * 1024 * 1024),
         name="second",
-    )(in_hbm(successor_ids), flow_v, cot_v, lines, mid, modes, msg, tables)
+    )(in_hbm(successor_ids), flow_v, cot_v, lines, mid, modes, msg, tables, sums)
 
     residual, grad = pl.pallas_call(
         kernel_blend,

time: 23.8 us -> 21.4 us (0.90)
  the two profiles are of different devices: /device:TPU:32 before, /device:TPU:64 now
where the time goes in v3:
time: 21.4 us; the launch traced here: 21.3 us
  Pallas kernels  10 us (47%)
  starting transfers between devices  9.29 us (43%)
  waiting for transfers between devices  1.33 us (6%)
  between operations  0.66 us (3%)
    ppermute x4, starting transfers between devices, swapped(): return lax.ppermute(value, axis, pairs)  9.29 us
    pallas_call x1, Pallas kernels, shards(): pl.pallas_call(kernel_first, out_shape=(shape(3, NQ, ROWS, 128), shape(6,...  6.43 us
    pallas_call x1, Pallas kernels, shards(): pl.pallas_call(kernel_second, out_shape=(shape(10, ROWS, 128), shape(10,...  2.42 us
    ppermute x4, waiting for transfers between devices, swapped(): return lax.ppermute(value, axis, pairs)  1.33 us
    pallas_call x1, Pallas kernels, shards(): pl.pallas_call(kernel_blend, out_shape=(shape(5, ROWS, 128), shape(5, ROW...  1.16 us
  transfers between devices with their start and end apart: 4, of which 1 were waited for; matrix products, arithmetic and copies ran while one was open for 0% of the time, Pallas kernels for 11%

profile of v3, /device:TPU:64, one launch (start us, length us, event | category | flops | bytes accessed | tf_op | source)
XLA Modules:
  0.0 21.3 jit_solution(11182526789049162575)
XLA Ops:
  0.6 6.4 %first.1 = (f32[3,13,128,128]{3,2,1,0:T(8,128)S(1)}, f32[6,175,8,128]{3,2,1,0:T(8,128)S(1)}, f32[128,128]{1,0:T(8,128)S(1)}, f32[16,128]{1,0:T(8,128)S(1)}, f32[...) custom-call(f32[5,128,128]{2,1,0:T(8,128)} %bitcast.5, ...), custom_call_target="tpu_custom_call" | custom-call | tf_op jit(solution)/shard_map/first/pallas_call | solution.py:742
  7.1 0.1 collective-permute-start
  7.2 4.1 %collective-permute-start.1 = (f32[168,128]{1,0:T(8,128)S(1)}, f32[168,128]{1,0:T(8,128)S(1)}, u32[]{:S(2)}, u32[]{:S(2)}) collective-permute-start(f32[168,128]{1,0:T(8,128)S(1)} %get-tuple-element.30), channel_id=1, source_target_pairs={{4,8},{8,4},{12,16},{16,12},{20,24},{24,20},{28,32},{32,28},{36,40... | collective-permute-start | bytes 258056 | tf_op jit(solution)/shard_map/ppermute | solution.py:721
  11.3 2.2 %collective-permute-start.2 = (f32[88,128]{1,0:T(8,128)S(1)}, f32[88,128]{1,0:T(8,128)S(1)}, u32[]{:S(2)}, u32[]{:S(2)}) collective-permute-start(f32[88,128]{1,0:T(8,128)S(1)} %get-tuple-element.31), channel_id=1, source_target_pairs={{0,1},{1,0},{2,3},{3,2},{4,5},{5,4},{6,7},{7,6},{8,9},{9,8},{10,11... | collective-permute-start | bytes 135176 | tf_op jit(solution)/shard_map/ppermute | solution.py:721
  13.5 2.9 %collective-permute-start.3 = (f32[88,128]{1,0:T(8,128)S(1)}, f32[88,128]{1,0:T(8,128)S(1)}, u32[]{:S(2)}, u32[]{:S(2)}) collective-permute-start(f32[88,128]{1,0:T(8,128)S(1)} %get-tuple-element.32), channel_id=1, source_target_pairs={{1,2},{2,1},{3,0},{0,3},{5,6},{6,5},{7,4},{4,7},{9,10},{10,9},{11,... | collective-permute-start | bytes 135176 | tf_op jit(solution)/shard_map/ppermute | solution.py:721
  16.4 2.4 %second.1 = (f32[10,128,128]{2,1,0:T(8,128)S(1)}, f32[10,128,128]{2,1,0:T(8,128)S(1)}, f32[5,128,128]{2,1,0:T(8,128)S(1)}, f32[8,128]{1,0:T(8,128)S(1)}, f32[3,20,128,128]{3,2,1,0:T(8,128)S(1)}) custom-call(s32[16]{0:T(128)} %ids_hbm.1, f32[5,128,128]{2,1,0:T(8,128)S(1)} %get-tuple-element.21.flow, ...), custom_call_target="tpu_custom_call", output_to_operand_aliasing={{4}: (8, {})} | custom-call | tf_op jit(solution)/shard_map/second/pallas_call | solution.py:777
  18.8 0.0 collective-permute-done.2.ahead
  18.8 1.3 %collective-permute-done.3.behind = f32[88,128]{1,0:T(8,128)S(1)} collective-permute-done((f32[88,128]{1,0:T(8,128)S(1)}, f32[88,128]{1,0:T(8,128)S(1)}, u32[]{:S(2)}, u32[]{:S(2)}) %collective-permute-start.3) | collective-permute-done | bytes 45088 | tf_op jit(solution)/shard_map/ppermute | solution.py:721
  20.1 0.0 collective-permute-done.partner
  20.1 0.0 collective-permute-done.1.other
  20.1 1.2 %blend.1 = (f32[5,128,128]{2,1,0:T(8,128)}, f32[5,128,128]{2,1,0:T(8,128)}) custom-call(f32[16,128]{1,0:T(8,128)S(1)} %get-tuple-element.20.msg, f32[8,128]{1,0:T(8,128)S(1)} %get-tuple-element.28.zsum, f32[168,128]{1,0:T(8,128)S(1)} %collective-permute-done.partner, f32[168,128]{1,0:T(8,128)S(1)} %collective-permute-done.1.other, ...), custom_call_target="tpu_custom_call" | custom-call | tf_op jit(solution)/shard_map/blend/pallas_call | solution.py:795
Async XLA Ops:
  7.1 13.1 %collective-permute-start = (f32[168,128]{1,0:T(8,128)S(1)}, f32[168,128]{1,0:T(8,128)S(1)}, u32[]{:S(2)}, u32[]{:S(2)}) collective-permute-start(f32[168,128]{1,0:T(8,128)S(1)} %get-tuple-element.29), channel_id=1, source_target_pairs={{0,4},{4,0},{8,12},{12,8},{16,20},{20,16},{24,28},{28,24},{32,36},... | collective-permute-start | bytes 258056 | tf_op jit(solution)/shard_map/ppermute | solution.py:721
  7.2 13.0 %collective-permute-start.1 = (f32[168,128]{1,0:T(8,128)S(1)}, f32[168,128]{1,0:T(8,128)S(1)}, u32[]{:S(2)}, u32[]{:S(2)}) collective-permute-start(f32[168,128]{1,0:T(8,128)S(1)} %get-tuple-element.30), channel_id=1, source_target_pairs={{4,8},{8,4},{12,16},{16,12},{20,24},{24,20},{28,32},{32,28},{36,40... | collective-permute-start | bytes 258056 | tf_op jit(solution)/shard_map/ppermute | solution.py:721
  11.3 7.5 %collective-permute-start.2 = (f32[88,128]{1,0:T(8,128)S(1)}, f32[88,128]{1,0:T(8,128)S(1)}, u32[]{:S(2)}, u32[]{:S(2)}) collective-permute-start(f32[88,128]{1,0:T(8,128)S(1)} %get-tuple-element.31), channel_id=1, source_target_pairs={{0,1},{1,0},{2,3},{3,2},{4,5},{5,4},{6,7},{7,6},{8,9},{9,8},{10,11... | collective-permute-start | bytes 135176 | tf_op jit(solution)/shard_map/ppermute | solution.py:721
  13.5 6.6 %collective-permute-start.3 = (f32[88,128]{1,0:T(8,128)S(1)}, f32[88,128]{1,0:T(8,128)S(1)}, u32[]{:S(2)}, u32[]{:S(2)}) collective-permute-start(f32[88,128]{1,0:T(8,128)S(1)} %get-tuple-element.32), channel_id=1, source_target_pairs={{1,2},{2,1},{3,0},{0,3},{5,6},{6,5},{7,4},{4,7},{9,10},{10,9},{11,... | collective-permute-start | bytes 135176 | tf_op jit(solution)/shard_map/ppermute | solution.py:721

commit v4 on v3

--- a/solution.py
+++ b/solution.py
@@ -285,13 +285,13 @@
             factors = jnp.where(sub16 == i + h, row, factors)
     msg[...] = factors
 
-    def one(step, carry):
+    def one(step):
         d = step // 2
         base = (step % 2) * 64
 
         def load(k):
-            rows = pl.ds(pl.multiple_of(base + 8 * k, 8), 8)
-            return [lines[d, q, rows, :] for q in range(NQ)]
+            start = base + 8 * k
+            return [lines[d, q, pl.ds(start, 8), :] for q in range(NQ)]
 
         gained = jnp.zeros((8, 128), F32)
         for k in range(7):
@@ -322,9 +322,9 @@
                     gained = gained + rate * (node.cot[q] - low.cot[q])
             low = node
         gsum[step] = gained
-        return carry
-
-    lax.fori_loop(0, 6, one, 0)
+
+    for step in range(6):
+        one(step)
 
     half_lane = lax.broadcasted_iota(jnp.int32, (16, 128), 1) >> 6
     along = jnp.concatenate([gsum[4], gsum[5]], axis=0)
@@ -372,8 +372,8 @@
 def steps_ahead():
     gx = lax.axis_index("gx")
     plane = 2 * lax.axis_index("gy") + gx // 32
-    corner = jnp.where(plane < 4, jnp.minimum(6 - plane, 5), 0)
-    return jnp.where(gx % 32 == 0, corner, jnp.where(plane < 2, 5 - plane, 0))
+    corner = jnp.where(plane < 4, 5 - plane, 0)
+    return jnp.where(gx % 32 == 0, corner, jnp.where(plane < 2, 4 - plane, 0))
 
 
 def adjoint_step(lines, mid, out, step):

time: 21.4 us -> 20.8 us (0.972); the launches traced: 21.3 us -> 20.4 us
  waiting for transfers between devices: 1.33 us -> 0.01 us
  starting transfers between devices: 9.29 us -> 9.93 us
  Pallas kernels: 10 us -> 9.78 us
    ppermute x4, waiting for transfers between devices: 1.33 us -> 0.01 us  [swapped(): return lax.ppermute(value, axis, pairs)]
    pallas_call x1, Pallas kernels: 6.43 us -> 5.57 us  [shards(): pl.pallas_call(kernel_first, out_shape=(shape(3, NQ, ROWS, 128), shape(6,...]
    ppermute x4, starting transfers between devices: 9.29 us -> 9.93 us  [swapped(): return lax.ppermute(value, axis, pairs)]
    pallas_call x1, Pallas kernels: 2.42 us -> 3.05 us  [shards(): pl.pallas_call(kernel_second, out_shape=(shape(10, ROWS, 128), shape(10,...]
  transfers between devices with their start and end apart: 4 -> 4, of which waited for: 1 -> 0; matrix products, arithmetic and copies ran while one was open for 0% -> 0% of each run, Pallas kernels for 11% -> 15%
where the time goes in v4:
time: 20.8 us; the launch traced here: 20.4 us
  starting transfers between devices  9.93 us (48%)
  Pallas kernels  9.78 us (47%)
  between operations  0.69 us (3%)
    ppermute x4, starting transfers between devices, swapped(): return lax.ppermute(value, axis, pairs)  9.93 us
    pallas_call x1, Pallas kernels, shards(): pl.pallas_call(kernel_first, out_shape=(shape(3, NQ, ROWS, 128), shape(6,...  5.57 us
    pallas_call x1, Pallas kernels, shards(): pl.pallas_call(kernel_second, out_shape=(shape(10, ROWS, 128), shape(10,...  3.05 us
    pallas_call x1, Pallas kernels, shards(): pl.pallas_call(kernel_blend, out_shape=(shape(5, ROWS, 128), shape(5, ROW...  1.16 us
  transfers between devices with their start and end apart: 4, of which 0 were waited for; matrix products, arithmetic and copies ran while one was open for 0% of the time, Pallas kernels for 15%

profile of v4, /device:TPU:64, one launch (start us, length us, event | category | flops | bytes accessed | tf_op | source)
XLA Modules:
  0.0 20.4 jit_solution(7783378630706570854)
XLA Ops:
  0.6 5.6 %first.1 = (f32[3,13,128,128]{3,2,1,0:T(8,128)S(1)}, f32[6,175,8,128]{3,2,1,0:T(8,128)S(1)}, f32[128,128]{1,0:T(8,128)S(1)}, f32[16,128]{1,0:T(8,128)S(1)}, f32[...) custom-call(f32[5,128,128]{2,1,0:T(8,128)} %bitcast.5, ...), custom_call_target="tpu_custom_call" | custom-call | tf_op jit(solution)/shard_map/first/pallas_call | solution.py:742
  6.2 0.1 collective-permute-start
  6.3 4.8 %collective-permute-start.1 = (f32[168,128]{1,0:T(8,128)S(1)}, f32[168,128]{1,0:T(8,128)S(1)}, u32[]{:S(2)}, u32[]{:S(2)}) collective-permute-start(f32[168,128]{1,0:T(8,128)S(1)} %get-tuple-element.30), channel_id=1, source_target_pairs={{4,8},{8,4},{12,16},{16,12},{20,24},{24,20},{28,32},{32,28},{36,40... | collective-permute-start | bytes 258056 | tf_op jit(solution)/shard_map/ppermute | solution.py:721
  11.1 1.5 %collective-permute-start.2 = (f32[88,128]{1,0:T(8,128)S(1)}, f32[88,128]{1,0:T(8,128)S(1)}, u32[]{:S(2)}, u32[]{:S(2)}) collective-permute-start(f32[88,128]{1,0:T(8,128)S(1)} %get-tuple-element.31), channel_id=1, source_target_pairs={{0,1},{1,0},{2,3},{3,2},{4,5},{5,4},{6,7},{7,6},{8,9},{9,8},{10,11... | collective-permute-start | bytes 135176 | tf_op jit(solution)/shard_map/ppermute | solution.py:721
  12.6 3.5 %collective-permute-start.3 = (f32[88,128]{1,0:T(8,128)S(1)}, f32[88,128]{1,0:T(8,128)S(1)}, u32[]{:S(2)}, u32[]{:S(2)}) collective-permute-start(f32[88,128]{1,0:T(8,128)S(1)} %get-tuple-element.32), channel_id=1, source_target_pairs={{1,2},{2,1},{3,0},{0,3},{5,6},{6,5},{7,4},{4,7},{9,10},{10,9},{11,... | collective-permute-start | bytes 135176 | tf_op jit(solution)/shard_map/ppermute | solution.py:721
  16.1 3.0 %second.1 = (f32[10,128,128]{2,1,0:T(8,128)S(1)}, f32[10,128,128]{2,1,0:T(8,128)S(1)}, f32[5,128,128]{2,1,0:T(8,128)S(1)}, f32[8,128]{1,0:T(8,128)S(1)}, f32[3,20,128,128]{3,2,1,0:T(8,128)S(1)}) custom-call(s32[16]{0:T(128)} %ids_hbm.1, f32[5,128,128]{2,1,0:T(8,128)S(1)} %get-tuple-element.21.flow, ...), custom_call_target="tpu_custom_call", output_to_operand_aliasing={{4}: (8, {})} | custom-call | tf_op jit(solution)/shard_map/second/pallas_call | solution.py:777
  19.2 0.0 collective-permute-done.2.ahead
  19.2 0.0 collective-permute-done.3.behind
  19.2 0.0 collective-permute-done.partner
  19.2 0.0 collective-permute-done.1.other
  19.2 1.2 %blend.1 = (f32[5,128,128]{2,1,0:T(8,128)}, f32[5,128,128]{2,1,0:T(8,128)}) custom-call(f32[16,128]{1,0:T(8,128)S(1)} %get-tuple-element.20.msg, f32[8,128]{1,0:T(8,128)S(1)} %get-tuple-element.28.zsum, f32[168,128]{1,0:T(8,128)S(1)} %collective-permute-done.partner, f32[168,128]{1,0:T(8,128)S(1)} %collective-permute-done.1.other, ...), custom_call_target="tpu_custom_call" | custom-call | tf_op jit(solution)/shard_map/blend/pallas_call | solution.py:795
Async XLA Ops:
  6.2 13.0 %collective-permute-start = (f32[168,128]{1,0:T(8,128)S(1)}, f32[168,128]{1,0:T(8,128)S(1)}, u32[]{:S(2)}, u32[]{:S(2)}) collective-permute-start(f32[168,128]{1,0:T(8,128)S(1)} %get-tuple-element.29), channel_id=1, source_target_pairs={{0,4},{4,0},{8,12},{12,8},{16,20},{20,16},{24,28},{28,24},{32,36},... | collective-permute-start | bytes 258056 | tf_op jit(solution)/shard_map/ppermute | solution.py:721
  6.3 12.9 %collective-permute-start.1 = (f32[168,128]{1,0:T(8,128)S(1)}, f32[168,128]{1,0:T(8,128)S(1)}, u32[]{:S(2)}, u32[]{:S(2)}) collective-permute-start(f32[168,128]{1,0:T(8,128)S(1)} %get-tuple-element.30), channel_id=1, source_target_pairs={{4,8},{8,4},{12,16},{16,12},{20,24},{24,20},{28,32},{32,28},{36,40... | collective-permute-start | bytes 258056 | tf_op jit(solution)/shard_map/ppermute | solution.py:721
  11.1 8.1 %collective-permute-start.2 = (f32[88,128]{1,0:T(8,128)S(1)}, f32[88,128]{1,0:T(8,128)S(1)}, u32[]{:S(2)}, u32[]{:S(2)}) collective-permute-start(f32[88,128]{1,0:T(8,128)S(1)} %get-tuple-element.31), channel_id=1, source_target_pairs={{0,1},{1,0},{2,3},{3,2},{4,5},{5,4},{6,7},{7,6},{8,9},{9,8},{10,11... | collective-permute-start | bytes 135176 | tf_op jit(solution)/shard_map/ppermute | solution.py:721
  12.6 6.6 %collective-permute-start.3 = (f32[88,128]{1,0:T(8,128)S(1)}, f32[88,128]{1,0:T(8,128)S(1)}, u32[]{:S(2)}, u32[]{:S(2)}) collective-permute-start(f32[88,128]{1,0:T(8,128)S(1)} %get-tuple-element.32), channel_id=1, source_target_pairs={{1,2},{2,1},{3,0},{0,3},{5,6},{6,5},{7,4},{4,7},{9,10},{10,9},{11,... | collective-permute-start | bytes 135176 | tf_op jit(solution)/shard_map/ppermute | solution.py:721

commit v5 on v4

--- a/solution.py
+++ b/solution.py
@@ -191,14 +191,20 @@
     copies = [
         pltpu.make_async_copy(source, target, sems.at[i])
         for i, (source, target) in enumerate(
-            ((flow_hbm, flow), (cot_hbm, cot), (tables_hbm, tables), (flags_hbm, flags))
+            (
+                (flow_hbm, flow),
+                (cot_hbm, cot),
+                (tables_hbm.at[pl.ds(0, 2)], tables.at[pl.ds(0, 2)]),
+                (flags_hbm, flags),
+                (tables_hbm.at[pl.ds(2, 2)], tables.at[pl.ds(2, 2)]),
+            )
         )
     ]
     for copy in copies:
         copy.start()
     even_x = lax.axis_index("gx") % 2 == 0
     even_y = lax.axis_index("gy") % 2 == 0
-    for copy in copies:
+    for copy in copies[:4]:
         copy.wait()
     for c in range(10):
         source, q = (flow, c) if c < 5 else (cot, c - 5)
@@ -345,6 +351,7 @@
         return carry
 
     lax.fori_loop(0, steps_ahead(), two, 0)
+    copies[4].wait()
 
 
 def conserved_node(state, cot, direction):
@@ -763,7 +770,7 @@
             pltpu.VMEM((ROWS, 128), F32),
             pltpu.VMEM((6, 8, 128), F32),
             pltpu.VMEM((2, 16), jnp.int32),
-            pltpu.SemaphoreType.DMA((4,)),
+            pltpu.SemaphoreType.DMA((5,)),
         ],
         compiler_params=pltpu.CompilerParams(vmem_limit_bytes=16 * 1024 * 1024),
         name="first",

time: 20.8 us -> 20.7 us (level)
  no operation moved by 1% of the time
where the time goes in v5:
time: 20.7 us; the launch traced here: 20.4 us
  starting transfers between devices  9.93 us (48%)
  Pallas kernels  9.75 us (47%)
  between operations  0.69 us (3%)
    ppermute x4, starting transfers between devices, swapped(): return lax.ppermute(value, axis, pairs)  9.93 us
    pallas_call x1, Pallas kernels, shards(): pl.pallas_call(kernel_first, out_shape=(shape(3, NQ, ROWS, 128), shape(6,...  5.54 us
    pallas_call x1, Pallas kernels, shards(): pl.pallas_call(kernel_second, out_shape=(shape(10, ROWS, 128), shape(10,...  3.05 us
    pallas_call x1, Pallas kernels, shards(): pl.pallas_call(kernel_blend, out_shape=(shape(5, ROWS, 128), shape(5, ROW...  1.16 us
  transfers between devices with their start and end apart: 4, of which 0 were waited for; matrix products, arithmetic and copies ran while one was open for 0% of the time, Pallas kernels for 15%

profile of v5, /device:TPU:64, one launch (start us, length us, event | category | flops | bytes accessed | tf_op | source)
XLA Modules:
  0.0 20.4 jit_solution(3460756792039685727)
XLA Ops:
  0.6 5.5 %first.1 = (f32[3,13,128,128]{3,2,1,0:T(8,128)S(1)}, f32[6,175,8,128]{3,2,1,0:T(8,128)S(1)}, f32[128,128]{1,0:T(8,128)S(1)}, f32[16,128]{1,0:T(8,128)S(1)}, f32[...) custom-call(f32[5,128,128]{2,1,0:T(8,128)} %bitcast.5, ...), custom_call_target="tpu_custom_call" | custom-call | tf_op jit(solution)/shard_map/first/pallas_call | solution.py:749
  6.2 0.1 collective-permute-start
  6.3 4.8 %collective-permute-start.1 = (f32[168,128]{1,0:T(8,128)S(1)}, f32[168,128]{1,0:T(8,128)S(1)}, u32[]{:S(2)}, u32[]{:S(2)}) collective-permute-start(f32[168,128]{1,0:T(8,128)S(1)} %get-tuple-element.30), channel_id=1, source_target_pairs={{4,8},{8,4},{12,16},{16,12},{20,24},{24,20},{28,32},{32,28},{36,40... | collective-permute-start | bytes 258056 | tf_op jit(solution)/shard_map/ppermute | solution.py:728
  11.1 1.5 %collective-permute-start.2 = (f32[88,128]{1,0:T(8,128)S(1)}, f32[88,128]{1,0:T(8,128)S(1)}, u32[]{:S(2)}, u32[]{:S(2)}) collective-permute-start(f32[88,128]{1,0:T(8,128)S(1)} %get-tuple-element.31), channel_id=1, source_target_pairs={{0,1},{1,0},{2,3},{3,2},{4,5},{5,4},{6,7},{7,6},{8,9},{9,8},{10,11... | collective-permute-start | bytes 135176 | tf_op jit(solution)/shard_map/ppermute | solution.py:728
  12.6 3.5 %collective-permute-start.3 = (f32[88,128]{1,0:T(8,128)S(1)}, f32[88,128]{1,0:T(8,128)S(1)}, u32[]{:S(2)}, u32[]{:S(2)}) collective-permute-start(f32[88,128]{1,0:T(8,128)S(1)} %get-tuple-element.32), channel_id=1, source_target_pairs={{1,2},{2,1},{3,0},{0,3},{5,6},{6,5},{7,4},{4,7},{9,10},{10,9},{11,... | collective-permute-start | bytes 135176 | tf_op jit(solution)/shard_map/ppermute | solution.py:728
  16.1 3.0 %second.1 = (f32[10,128,128]{2,1,0:T(8,128)S(1)}, f32[10,128,128]{2,1,0:T(8,128)S(1)}, f32[5,128,128]{2,1,0:T(8,128)S(1)}, f32[8,128]{1,0:T(8,128)S(1)}, f32[3,20,128,128]{3,2,1,0:T(8,128)S(1)}) custom-call(s32[16]{0:T(128)} %ids_hbm.1, f32[5,128,128]{2,1,0:T(8,128)S(1)} %get-tuple-element.21.flow, ...), custom_call_target="tpu_custom_call", output_to_operand_aliasing={{4}: (8, {})} | custom-call | tf_op jit(solution)/shard_map/second/pallas_call | solution.py:784
  19.2 0.0 collective-permute-done.2.ahead
  19.2 0.0 collective-permute-done.3.behind
  19.2 0.0 collective-permute-done.partner
  19.2 0.0 collective-permute-done.1.other
  19.2 1.2 %blend.1 = (f32[5,128,128]{2,1,0:T(8,128)}, f32[5,128,128]{2,1,0:T(8,128)}) custom-call(f32[16,128]{1,0:T(8,128)S(1)} %get-tuple-element.20.msg, f32[8,128]{1,0:T(8,128)S(1)} %get-tuple-element.28.zsum, f32[168,128]{1,0:T(8,128)S(1)} %collective-permute-done.partner, f32[168,128]{1,0:T(8,128)S(1)} %collective-permute-done.1.other, ...), custom_call_target="tpu_custom_call" | custom-call | tf_op jit(solution)/shard_map/blend/pallas_call | solution.py:802
Async XLA Ops:
  6.2 13.0 %collective-permute-start = (f32[168,128]{1,0:T(8,128)S(1)}, f32[168,128]{1,0:T(8,128)S(1)}, u32[]{:S(2)}, u32[]{:S(2)}) collective-permute-start(f32[168,128]{1,0:T(8,128)S(1)} %get-tuple-element.29), channel_id=1, source_target_pairs={{0,4},{4,0},{8,12},{12,8},{16,20},{20,16},{24,28},{28,24},{32,36},... | collective-permute-start | bytes 258056 | tf_op jit(solution)/shard_map/ppermute | solution.py:728
  6.3 12.9 %collective-permute-start.1 = (f32[168,128]{1,0:T(8,128)S(1)}, f32[168,128]{1,0:T(8,128)S(1)}, u32[]{:S(2)}, u32[]{:S(2)}) collective-permute-start(f32[168,128]{1,0:T(8,128)S(1)} %get-tuple-element.30), channel_id=1, source_target_pairs={{4,8},{8,4},{12,16},{16,12},{20,24},{24,20},{28,32},{32,28},{36,40... | collective-permute-start | bytes 258056 | tf_op jit(solution)/shard_map/ppermute | solution.py:728
  11.1 8.1 %collective-permute-start.2 = (f32[88,128]{1,0:T(8,128)S(1)}, f32[88,128]{1,0:T(8,128)S(1)}, u32[]{:S(2)}, u32[]{:S(2)}) collective-permute-start(f32[88,128]{1,0:T(8,128)S(1)} %get-tuple-element.31), channel_id=1, source_target_pairs={{0,1},{1,0},{2,3},{3,2},{4,5},{5,4},{6,7},{7,6},{8,9},{9,8},{10,11... | collective-permute-start | bytes 135176 | tf_op jit(solution)/shard_map/ppermute | solution.py:728
  12.6 6.6 %collective-permute-start.3 = (f32[88,128]{1,0:T(8,128)S(1)}, f32[88,128]{1,0:T(8,128)S(1)}, u32[]{:S(2)}, u32[]{:S(2)}) collective-permute-start(f32[88,128]{1,0:T(8,128)S(1)} %get-tuple-element.32), channel_id=1, source_target_pairs={{1,2},{2,1},{3,0},{0,3},{5,6},{6,5},{7,4},{4,7},{9,10},{10,9},{11,... | collective-permute-start | bytes 135176 | tf_op jit(solution)/shard_map/ppermute | solution.py:728
